TPU v7x, 32 devices: a whole 2x2x4 slice. The times are simulated.
32 devices in a mesh: section: 4 (over y, core), dp: 8 (over z, x).
Axes of the slice: x: 2, y: 2, z: 4, core: 2. Of those that a mesh axis runs over, the one named last changes fastest.
Arguments:
- embeds: bfloat16 [64, 197, 768], P('dp'), may hold values from -6 to 6
- mask: int32 [64, 197], P('dp'), may hold values from 0 to 1, as said below
- cotangent: bfloat16 [64, 197, 768], P('dp'), may hold values from -6 to 6
- section_weight: bfloat16 [4, 768, 3072], P('section')
- down_weight: bfloat16 [4, 3072, 768], P('section'), may hold values from -0.109375 to 0.109375
- section_vectors: float32 [4, 8, 768], P('section')
- rel_table: float32 [4, 12, 732], P('section'), may hold values from -4 to 4
Outputs:
- activations: bfloat16 [4, 64, 197, 768], P('section', 'dp')
- input_grads: float32 [4, 64, 197, 768], P('section', 'dp')
- grad_weight: float32 [4, 768, 3072], P('section')
- grad_down: float32 [4, 3072, 768], P('section')
- grad_vectors: float32 [4, 8, 768], P('section')
- grad_table: float32 [4, 12, 732], P('section')
Inputs may be any that keep to these rules, and one draw needn't show every extreme that they name: `mask`: column 0 (class row) is 0. Each image masks between 40 and 110 of its patches as one compact block around a centre; some image masks exactly 110 and another exactly 40.
All inputs are finite; a program needn't handle non-finite values.
Results may differ from a plain program's by a relative error of at most 0.015.
Values may be sent and summed in bfloat16 or wider, within the bound.
No kernel may reach another device: no remote copies, remote signals or barrier semaphores. Data moves between devices by JAX's collectives and lax.ppermute only.
A program may use at most 192 MiB of HBM per device.

v0:
```python
from functools import partial

import jax
import jax.numpy as jnp
from jax import lax
from jax.sharding import PartitionSpec as P

GRID = 14


EPS = 1e-06


def from_behind(block, axis, distance):
    devices = range(lax.axis_size(axis))
    route = [(i - distance, i) for i in devices if i - distance in devices]
    return lax.ppermute(block, axis, route)


def norm_rows(values, gain, shift):
    center = values - jnp.mean(values, -1, keepdims=True)
    spread = jnp.mean(center * center, -1, keepdims=True)
    return center * lax.rsqrt(spread + EPS) * gain + shift


def relative_index(grid):
    side_len = 2 * grid - 1
    total = side_len * side_len + 3
    places = jnp.arange(grid * grid, dtype=jnp.int32)
    row_of = places // grid
    col_of = places % grid
    patch_part = (row_of[:, None] - row_of[None, :] + grid - 1) * side_len + (
        col_of[:, None] - col_of[None, :] + grid - 1
    )
    top_row = jnp.full((1, grid * grid), total - 3, jnp.int32)
    left_col = jnp.full((grid * grid, 1), total - 2, jnp.int32)
    corner = jnp.full((1, 1), total - 1, jnp.int32)
    upper = jnp.concatenate([corner, top_row], 1)
    lower_part = jnp.concatenate([left_col, patch_part], 1)
    return jnp.concatenate([upper, lower_part], 0)


def offset_table(grid):
    first = lax.broadcasted_iota(jnp.int32, (grid, grid, 2 * grid - 1), 0)
    second = lax.broadcasted_iota(jnp.int32, (grid, grid, 2 * grid - 1), 1)
    target = lax.broadcasted_iota(jnp.int32, (grid, grid, 2 * grid - 1), 2)
    return (first - second + grid - 1 == target).astype(jnp.float32)


def table_grad(grad_scores, grid):
    head_count = grad_scores.shape[0]
    offsets = offset_table(grid)
    patch_block = grad_scores[:, 1:, 1:].reshape(head_count, grid, grid, grid, grid)
    by_rows = jnp.einsum("hrcsd,rsa->hacd", patch_block, offsets, precision=lax.Precision.HIGHEST)
    by_both = jnp.einsum("hacd,cdb->hab", by_rows, offsets, precision=lax.Precision.HIGHEST)
    to_patch = jnp.sum(grad_scores[:, 0, 1:], 1)
    to_class = jnp.sum(grad_scores[:, 1:, 0], 1)
    self_term = grad_scores[:, 0, 0]
    tail = jnp.stack([to_patch, to_class, self_term], 1)
    return jnp.concatenate([by_both.reshape(head_count, -1), tail], 1)


def matmul(left, right):
    return jnp.dot(left, right, preferred_element_type=jnp.float32)


def left_t(left, right):
    return lax.dot_general(
        left, right, (((0,), (0,)), ((), ())), preferred_element_type=jnp.float32
    )


def right_t(left, right):
    return lax.dot_general(
        left, right, (((1,), (1,)), ((), ())), preferred_element_type=jnp.float32
    )


def attend_parts(stream, matrix, vectors, position_bias):
    length, width = stream.shape
    head_count = position_bias.shape[0]
    normed, norm_pull = jax.vjp(norm_rows, stream, vectors[0], vectors[1])
    inputs = normed.astype(jnp.bfloat16)
    joined = matmul(inputs, matrix[:, : 3 * width])
    queries = (joined[:, :width] + vectors[4]).astype(jnp.bfloat16).reshape(length, head_count, -1)
    key_rows = joined[:, width : 2 * width].astype(jnp.bfloat16).reshape(length, head_count, -1)
    value_rows = (
        (joined[:, 2 * width :] + vectors[5]).astype(jnp.bfloat16).reshape(length, head_count, -1)
    )
    factor = queries.shape[2] ** (-0.5)
    scores = (
        jnp.einsum("qhd,khd->hqk", queries, key_rows, preferred_element_type=jnp.float32) * factor
        + position_bias
    )
    softened, soft_pull = jax.vjp(partial(jax.nn.softmax, axis=-1), scores)
    weights_low = softened.astype(jnp.bfloat16)
    context = jnp.einsum(
        "hqk,khd->qhd", weights_low, value_rows, preferred_element_type=jnp.float32
    )
    context = context.reshape(length, width).astype(jnp.bfloat16)
    branch = matmul(context, matrix[:, 3 * width :]) + vectors[3]
    output = stream + vectors[2] * branch
    saved = (
        norm_pull,
        inputs,
        queries,
        key_rows,
        value_rows,
        factor,
        soft_pull,
        weights_low,
        context,
        branch,
    )
    return (output, saved)


def attend_back(stream, grad_out, totals, matrix, vectors, position_bias):
    output, saved = attend_parts(stream, matrix, vectors, position_bias)
    (
        norm_pull,
        inputs,
        queries,
        key_rows,
        value_rows,
        factor,
        soft_pull,
        weights_low,
        context,
        branch,
    ) = saved
    length, width = stream.shape
    head_count = position_bias.shape[0]
    grad_matrix, grad_lower, grad_rows, grad_bias = totals
    scaled = vectors[2] * grad_out
    scaled_low = scaled.astype(jnp.bfloat16)
    grad_proj_out = left_t(context, scaled_low)
    grad_context = (
        right_t(scaled_low, matrix[:, 3 * width :])
        .astype(jnp.bfloat16)
        .reshape(length, head_count, -1)
    )
    grad_weights = jnp.einsum(
        "qhd,khd->hqk", grad_context, value_rows, preferred_element_type=jnp.float32
    )
    grad_values = jnp.einsum(
        "hqk,qhd->khd", weights_low, grad_context, preferred_element_type=jnp.float32
    ).reshape(length, width)
    (grad_scores,) = soft_pull(grad_weights)
    grad_table = table_grad(grad_scores, GRID)
    grad_logits = (grad_scores * factor).astype(jnp.bfloat16)
    grad_queries = jnp.einsum(
        "hqk,khd->qhd", grad_logits, key_rows, preferred_element_type=jnp.float32
    ).reshape(length, width)
    grad_keys = jnp.einsum(
        "hqk,qhd->khd", grad_logits, queries, preferred_element_type=jnp.float32
    ).reshape(length, width)
    grad_joined = jnp.concatenate([grad_queries, grad_keys, grad_values], 1).astype(jnp.bfloat16)
    grad_proj_in = left_t(inputs, grad_joined)
    grad_inputs = right_t(grad_joined, matrix[:, : 3 * width])
    grad_stream, grad_gain, grad_shift = norm_pull(grad_inputs)
    nothing = jnp.zeros_like(grad_gain)
    row_terms = jnp.stack(
        [
            grad_gain,
            grad_shift,
            jnp.sum(grad_out * branch, 0),
            jnp.sum(scaled, 0),
            jnp.sum(grad_queries, 0),
            jnp.sum(grad_values, 0),
            nothing,
            nothing,
        ]
    )
    grad_matrix = grad_matrix + jnp.concatenate([grad_proj_in, grad_proj_out], 1)
    return (
        grad_out + grad_stream,
        (grad_matrix, grad_lower, grad_rows + row_terms, grad_bias + grad_table),
    )


def feed_parts(stream, matrix, down_matrix, vectors):
    normed, norm_pull = jax.vjp(norm_rows, stream, vectors[0], vectors[1])
    inputs = normed.astype(jnp.bfloat16)
    hidden = matmul(inputs, matrix) + vectors[4:].reshape(-1)
    active, gelu_pull = jax.vjp(partial(jax.nn.gelu, approximate=False), hidden)
    active_low = active.astype(jnp.bfloat16)
    branch = matmul(active_low, down_matrix) + vectors[3]
    output = stream + vectors[2] * branch
    return (output, (norm_pull, inputs, gelu_pull, active_low, branch))


def feed_back(stream, grad_out, totals, matrix, down_matrix, vectors):
    output, saved = feed_parts(stream, matrix, down_matrix, vectors)
    norm_pull, inputs, gelu_pull, active_low, branch = saved
    grad_matrix, grad_lower, grad_rows, grad_bias = totals
    width = stream.shape[1]
    scaled = vectors[2] * grad_out
    scaled_low = scaled.astype(jnp.bfloat16)
    grad_lower = grad_lower + left_t(active_low, scaled_low)
    grad_active = right_t(scaled_low, down_matrix)
    (grad_hidden,) = gelu_pull(grad_active)
    hidden_low = grad_hidden.astype(jnp.bfloat16)
    grad_matrix = grad_matrix + left_t(inputs, hidden_low)
    grad_inputs = right_t(hidden_low, matrix)
    grad_stream, grad_gain, grad_shift = norm_pull(grad_inputs)
    head_rows = jnp.stack(
        [grad_gain, grad_shift, jnp.sum(grad_out * branch, 0), jnp.sum(scaled, 0)]
    )
    row_terms = jnp.concatenate([head_rows, jnp.sum(grad_hidden, 0).reshape(4, width)], 0)
    return (grad_out + grad_stream, (grad_matrix, grad_lower, grad_rows + row_terms, grad_bias))


def store_at(buffer, update, place, valid):
    previous = lax.dynamic_index_in_dim(buffer, place, 0, False)
    return lax.dynamic_update_index_in_dim(buffer, jnp.where(valid, update, previous), place, 0)


def on_device(embeds, mask, cotangent, section_weight, down_weight, section_vectors, rel_table):
    sections = lax.axis_size("section")
    section_now = lax.axis_index("section")
    images = embeds.shape[0]
    matrix = section_weight[0]
    down_matrix = down_weight[0]
    vectors = section_vectors[0]
    rel_bias = rel_table[0]
    lookup = relative_index(GRID)
    position_bias = rel_bias[:, lookup]
    is_feed = section_now % 2 == 1
    first = section_now == 0
    final = section_now == sections - 1
    cover = mask.astype(jnp.float32)[:, :, None]
    start = embeds.astype(jnp.float32) * (1.0 - cover) + vectors[6] * cover

    def forward_one(stream):
        return lax.cond(
            is_feed,
            lambda inner: feed_parts(inner, matrix, down_matrix, vectors)[0],
            lambda inner: attend_parts(inner, matrix, vectors, position_bias)[0],
            stream,
        )

    def backward_one(stream, grad_out, totals):
        return lax.cond(
            is_feed,
            lambda inner, upper, sums: feed_back(inner, upper, sums, matrix, down_matrix, vectors),
            lambda inner, upper, sums: attend_back(
                inner, upper, sums, matrix, vectors, position_bias
            ),
            stream,
            grad_out,
            totals,
        )

    ticks = images + sections - 1

    def forward_tick(carry, tick):
        incoming, kept, sent_all = carry
        slot = tick - section_now
        valid = (slot >= 0) & (slot < images)
        place = jnp.clip(slot, 0, images - 1)
        stream = jnp.where(
            first, lax.dynamic_index_in_dim(start, place, 0, False), incoming.astype(jnp.float32)
        )
        sent = forward_one(stream).astype(jnp.bfloat16)
        kept = store_at(kept, stream, place, valid)
        sent_all = store_at(sent_all, sent, place, valid)
        incoming = from_behind(sent, "section", 1)
        return ((incoming, kept, sent_all), None)

    blank = jnp.zeros(embeds.shape, jnp.bfloat16)
    (unused_in, kept, sent_all), unused_out = lax.scan(
        forward_tick, (blank[0], jnp.zeros(embeds.shape, jnp.float32), blank), jnp.arange(ticks)
    )
    zero_totals = (
        jnp.zeros(matrix.shape, jnp.float32),
        jnp.zeros(down_matrix.shape, jnp.float32),
        jnp.zeros(vectors.shape, jnp.float32),
        jnp.zeros(rel_bias.shape, jnp.float32),
    )

    def chain_tick(carry, tick):
        incoming, grads_in, totals, grad_store = carry
        slot = tick - (sections - 1 - section_now)
        valid = (slot >= 0) & (slot < images)
        place = jnp.clip(slot, 0, images - 1)
        stream = lax.dynamic_index_in_dim(kept, place, 0, False)
        grad_out = jnp.where(
            final,
            lax.dynamic_index_in_dim(cotangent, place, 0, False).astype(jnp.float32),
            incoming.astype(jnp.float32),
        )
        grad_out = jnp.where(valid, grad_out, 0.0)
        grad_stream, totals = backward_one(stream, grad_out, totals)
        grads_in = store_at(grads_in, grad_stream, place, valid)
        incoming = from_behind(grad_stream.astype(jnp.bfloat16), "section", -1)
        return ((incoming, grads_in, totals, grad_store), None)

    zeros_f = jnp.zeros(embeds.shape, jnp.float32)
    (unused_in, grads_in, totals, grad_store), unused_out = lax.scan(
        chain_tick, (blank[0], zeros_f, zero_totals, zeros_f), jnp.arange(ticks)
    )
    token_grad = jnp.sum(grads_in * cover, (0, 1))
    grad_matrix, grad_lower, grad_rows, grad_bias = totals
    grad_rows = grad_rows.at[6].add(jnp.where(first, token_grad, 0.0))
    summed = lax.psum((grad_matrix, grad_lower, grad_rows, grad_bias), "dp")
    input_grads = jnp.where(first, grads_in * (1.0 - cover), grads_in)
    return (
        sent_all[None],
        input_grads[None],
        summed[0][None],
        summed[1][None],
        summed[2][None],
        summed[3][None],
    )


def solution(mesh):
    placed = (
        P("dp", None, None),
        P("dp", None),
        P("dp", None, None),
        P("section", None, None),
        P("section", None, None),
        P("section", None, None),
        P("section", None, None),
    )
    return jax.shard_map(
        on_device,
        mesh=mesh,
        in_specs=placed,
        out_specs=(
            P("section", "dp", None, None),
            P("section", "dp", None, None),
            P("section", None, None),
            P("section", None, None),
            P("section", None, None),
            P("section", None, None),
        ),
        check_vma=False,
    )
```

profile of v0, /device:TPU:1, one launch (start us, length us, event | category | flops | bytes accessed | tf_op | source)
XLA Modules:
  0.0 2451.0 jit_solution(16344209484714883210)
XLA Ops:
  12.0 128.5 %gather_fusion = f32[38809,12]{1,0:T(8,128)} fusion(f32[12,732]{0,1:T(8,128)S(1)} %bitcast.148, s32[38912]{0:T(1024)S(1)} %pad_clamp_fusion), kind=kCustom, calls=%fused_computation | custom fusion | bytes 3880900 | tf_op jit(solution)/shard_map/gather | solution.py:228
  167.2 292.3 %while.37 = (s32[]{:T(128)}, bf16[197,768]{1,0:T(8,128)(2,1)S(1)}, f32[8,197,768]{2,1,0:T(8,128)}, bf16[8,197,768]{2,1,0:T(8,128)(2,1)}, pred[]{:T(512)}, /*inde...) while((s32[]{:T(128)}, bf16[197,768]{1,0:T(8,128)(2,1)S(1)}, ...), condition=%wide.region_9.10_spmd, body=%wide.region_0.9_spmd.sunk | while | flops 1901639680 | bytes 31722464 | solution.py:272
  471.9 1381.1 %while.38 = (s32[]{:T(128)}, bf16[197,768]{1,0:T(8,128)(2,1)S(1)}, f32[8,197,768]{2,0,1:T(8,128)}, f32[768,3072]{1,0:T(8,128)}, f32[3072,768]{1,0:T(8,128)}, /*i...) while((s32[]{:T(128)}, bf16[197,768]{1,0:T(8,128)(2,1)S(1)}, ...), condition=%wide.region_37.38_spmd, body=%wide.region_10.37_spmd.sunk | while | flops 5638075392 | bytes 143024208 | solution.py:300
  501.2 35.4 %conditional.10 = (f32[197,768]{1,0:T(8,128)}, f32[768,3072]{1,0:T(8,128)}, f32[3072,768]{1,0:T(8,128)}, f32[8,768]{1,0:T(8,128)S(1)}, f32[12,732]{1,0:T(8,128)}) conditional(s32[]{:T(128)} %convert_element_type.186, (f32[197,768]{1,0:T(8,128)S(1)}, f32[8,768]{1,0:T(8,128)S(1)}, bf16[768,3072]{1,0:T(8,128)(2,1)}, f32[197,768]{1,0:T(8,128)S(1)}, ...), branch_computations={%region_11.26_spmd, %region_27.36_spmd} | conditional | flops 5637167616 | bytes 133643008 | solution.py:244
  538.2 61.9 %collective-permute-start.1 = (bf16[197,768]{1,0:T(8,128)(2,1)S(1)}, bf16[197,768]{1,0:T(8,128)(2,1)S(1)}, u32[]{:S(2)}, u32[]{:S(2)}) collective-permute-start(bf16[197,768]{1,0:T(8,128)(2,1)S(1)} %get-tuple-element.771), channel_id=1, source_target_pairs={{8,0},{16,8},{24,16},{9,1},{17,9},{25,17},{10,2},{18,10},{26,18},{... | collective-permute-start | bytes 907784 | tf_op jit(solution)/shard_map/while/body/eval_jaxpr/ppermute | solution.py:17
  600.8 12.5 dynamic_update_slice.20
  620.3 35.4 %conditional.10 = (f32[197,768]{1,0:T(8,128)}, f32[768,3072]{1,0:T(8,128)}, f32[3072,768]{1,0:T(8,128)}, f32[8,768]{1,0:T(8,128)S(1)}, f32[12,732]{1,0:T(8,128)}) conditional(s32[]{:T(128)} %convert_element_type.186, (f32[197,768]{1,0:T(8,128)S(1)}, f32[8,768]{1,0:T(8,128)S(1)}, bf16[768,3072]{1,0:T(8,128)(2,1)}, f32[197,768]{1,0:T(8,128)S(1)}, ...), branch_computations={%region_11.26_spmd, %region_27.36_spmd} | conditional | flops 5637167616 | bytes 133643008 | solution.py:244
  657.3 66.3 %collective-permute-start.1 = (bf16[197,768]{1,0:T(8,128)(2,1)S(1)}, bf16[197,768]{1,0:T(8,128)(2,1)S(1)}, u32[]{:S(2)}, u32[]{:S(2)}) collective-permute-start(bf16[197,768]{1,0:T(8,128)(2,1)S(1)} %get-tuple-element.771), channel_id=1, source_target_pairs={{8,0},{16,8},{24,16},{9,1},{17,9},{25,17},{10,2},{18,10},{26,18},{... | collective-permute-start | bytes 907784 | tf_op jit(solution)/shard_map/while/body/eval_jaxpr/ppermute | solution.py:17
  724.2 12.5 dynamic_update_slice.20
  743.8 35.4 %conditional.10 = (f32[197,768]{1,0:T(8,128)}, f32[768,3072]{1,0:T(8,128)}, f32[3072,768]{1,0:T(8,128)}, f32[8,768]{1,0:T(8,128)S(1)}, f32[12,732]{1,0:T(8,128)}) conditional(s32[]{:T(128)} %convert_element_type.186, (f32[197,768]{1,0:T(8,128)S(1)}, f32[8,768]{1,0:T(8,128)S(1)}, bf16[768,3072]{1,0:T(8,128)(2,1)}, f32[197,768]{1,0:T(8,128)S(1)}, ...), branch_computations={%region_11.26_spmd, %region_27.36_spmd} | conditional | flops 5637167616 | bytes 133643008 | solution.py:244
  780.8 66.3 %collective-permute-start.1 = (bf16[197,768]{1,0:T(8,128)(2,1)S(1)}, bf16[197,768]{1,0:T(8,128)(2,1)S(1)}, u32[]{:S(2)}, u32[]{:S(2)}) collective-permute-start(bf16[197,768]{1,0:T(8,128)(2,1)S(1)} %get-tuple-element.771), channel_id=1, source_target_pairs={{8,0},{16,8},{24,16},{9,1},{17,9},{25,17},{10,2},{18,10},{26,18},{... | collective-permute-start | bytes 907784 | tf_op jit(solution)/shard_map/while/body/eval_jaxpr/ppermute | solution.py:17
  847.7 12.5 dynamic_update_slice.20
  867.4 35.4 %conditional.10 = (f32[197,768]{1,0:T(8,128)}, f32[768,3072]{1,0:T(8,128)}, f32[3072,768]{1,0:T(8,128)}, f32[8,768]{1,0:T(8,128)S(1)}, f32[12,732]{1,0:T(8,128)}) conditional(s32[]{:T(128)} %convert_element_type.186, (f32[197,768]{1,0:T(8,128)S(1)}, f32[8,768]{1,0:T(8,128)S(1)}, bf16[768,3072]{1,0:T(8,128)(2,1)}, f32[197,768]{1,0:T(8,128)S(1)}, ...), branch_computations={%region_11.26_spmd, %region_27.36_spmd} | conditional | flops 5637167616 | bytes 133643008 | solution.py:244
  904.3 66.2 %collective-permute-start.1 = (bf16[197,768]{1,0:T(8,128)(2,1)S(1)}, bf16[197,768]{1,0:T(8,128)(2,1)S(1)}, u32[]{:S(2)}, u32[]{:S(2)}) collective-permute-start(bf16[197,768]{1,0:T(8,128)(2,1)S(1)} %get-tuple-element.771), channel_id=1, source_target_pairs={{8,0},{16,8},{24,16},{9,1},{17,9},{25,17},{10,2},{18,10},{26,18},{... | collective-permute-start | bytes 907784 | tf_op jit(solution)/shard_map/while/body/eval_jaxpr/ppermute | solution.py:17
  971.2 12.5 dynamic_update_slice.20
  991.5 35.4 %conditional.10 = (f32[197,768]{1,0:T(8,128)}, f32[768,3072]{1,0:T(8,128)}, f32[3072,768]{1,0:T(8,128)}, f32[8,768]{1,0:T(8,128)S(1)}, f32[12,732]{1,0:T(8,128)}) conditional(s32[]{:T(128)} %convert_element_type.186, (f32[197,768]{1,0:T(8,128)S(1)}, f32[8,768]{1,0:T(8,128)S(1)}, bf16[768,3072]{1,0:T(8,128)(2,1)}, f32[197,768]{1,0:T(8,128)S(1)}, ...), branch_computations={%region_11.26_spmd, %region_27.36_spmd} | conditional | flops 5637167616 | bytes 133643008 | solution.py:244
  1028.4 65.5 %collective-permute-start.1 = (bf16[197,768]{1,0:T(8,128)(2,1)S(1)}, bf16[197,768]{1,0:T(8,128)(2,1)S(1)}, u32[]{:S(2)}, u32[]{:S(2)}) collective-permute-start(bf16[197,768]{1,0:T(8,128)(2,1)S(1)} %get-tuple-element.771), channel_id=1, source_target_pairs={{8,0},{16,8},{24,16},{9,1},{17,9},{25,17},{10,2},{18,10},{26,18},{... | collective-permute-start | bytes 907784 | tf_op jit(solution)/shard_map/while/body/eval_jaxpr/ppermute | solution.py:17
  1115.5 35.4 %conditional.10 = (f32[197,768]{1,0:T(8,128)}, f32[768,3072]{1,0:T(8,128)}, f32[3072,768]{1,0:T(8,128)}, f32[8,768]{1,0:T(8,128)S(1)}, f32[12,732]{1,0:T(8,128)}) conditional(s32[]{:T(128)} %convert_element_type.186, (f32[197,768]{1,0:T(8,128)S(1)}, f32[8,768]{1,0:T(8,128)S(1)}, bf16[768,3072]{1,0:T(8,128)(2,1)}, f32[197,768]{1,0:T(8,128)S(1)}, ...), branch_computations={%region_11.26_spmd, %region_27.36_spmd} | conditional | flops 5637167616 | bytes 133643008 | solution.py:244
  1152.5 64.9 %collective-permute-start.1 = (bf16[197,768]{1,0:T(8,128)(2,1)S(1)}, bf16[197,768]{1,0:T(8,128)(2,1)S(1)}, u32[]{:S(2)}, u32[]{:S(2)}) collective-permute-start(bf16[197,768]{1,0:T(8,128)(2,1)S(1)} %get-tuple-element.771), channel_id=1, source_target_pairs={{8,0},{16,8},{24,16},{9,1},{17,9},{25,17},{10,2},{18,10},{26,18},{... | collective-permute-start | bytes 907784 | tf_op jit(solution)/shard_map/while/body/eval_jaxpr/ppermute | solution.py:17
  1239.6 35.4 %conditional.10 = (f32[197,768]{1,0:T(8,128)}, f32[768,3072]{1,0:T(8,128)}, f32[3072,768]{1,0:T(8,128)}, f32[8,768]{1,0:T(8,128)S(1)}, f32[12,732]{1,0:T(8,128)}) conditional(s32[]{:T(128)} %convert_element_type.186, (f32[197,768]{1,0:T(8,128)S(1)}, f32[8,768]{1,0:T(8,128)S(1)}, bf16[768,3072]{1,0:T(8,128)(2,1)}, f32[197,768]{1,0:T(8,128)S(1)}, ...), branch_computations={%region_11.26_spmd, %region_27.36_spmd} | conditional | flops 5637167616 | bytes 133643008 | solution.py:244
  1276.6 64.3 %collective-permute-start.1 = (bf16[197,768]{1,0:T(8,128)(2,1)S(1)}, bf16[197,768]{1,0:T(8,128)(2,1)S(1)}, u32[]{:S(2)}, u32[]{:S(2)}) collective-permute-start(bf16[197,768]{1,0:T(8,128)(2,1)S(1)} %get-tuple-element.771), channel_id=1, source_target_pairs={{8,0},{16,8},{24,16},{9,1},{17,9},{25,17},{10,2},{18,10},{26,18},{... | collective-permute-start | bytes 907784 | tf_op jit(solution)/shard_map/while/body/eval_jaxpr/ppermute | solution.py:17
  1341.5 12.5 dynamic_update_slice.20
  1363.7 35.4 %conditional.10 = (f32[197,768]{1,0:T(8,128)}, f32[768,3072]{1,0:T(8,128)}, f32[3072,768]{1,0:T(8,128)}, f32[8,768]{1,0:T(8,128)S(1)}, f32[12,732]{1,0:T(8,128)}) conditional(s32[]{:T(128)} %convert_element_type.186, (f32[197,768]{1,0:T(8,128)S(1)}, f32[8,768]{1,0:T(8,128)S(1)}, bf16[768,3072]{1,0:T(8,128)(2,1)}, f32[197,768]{1,0:T(8,128)S(1)}, ...), branch_computations={%region_11.26_spmd, %region_27.36_spmd} | conditional | flops 5637167616 | bytes 133643008 | solution.py:244
  1400.7 63.6 %collective-permute-start.1 = (bf16[197,768]{1,0:T(8,128)(2,1)S(1)}, bf16[197,768]{1,0:T(8,128)(2,1)S(1)}, u32[]{:S(2)}, u32[]{:S(2)}) collective-permute-start(bf16[197,768]{1,0:T(8,128)(2,1)S(1)} %get-tuple-element.771), channel_id=1, source_target_pairs={{8,0},{16,8},{24,16},{9,1},{17,9},{25,17},{10,2},{18,10},{26,18},{... | collective-permute-start | bytes 907784 | tf_op jit(solution)/shard_map/while/body/eval_jaxpr/ppermute | solution.py:17
  1487.8 35.4 %conditional.10 = (f32[197,768]{1,0:T(8,128)}, f32[768,3072]{1,0:T(8,128)}, f32[3072,768]{1,0:T(8,128)}, f32[8,768]{1,0:T(8,128)S(1)}, f32[12,732]{1,0:T(8,128)}) conditional(s32[]{:T(128)} %convert_element_type.186, (f32[197,768]{1,0:T(8,128)S(1)}, f32[8,768]{1,0:T(8,128)S(1)}, bf16[768,3072]{1,0:T(8,128)(2,1)}, f32[197,768]{1,0:T(8,128)S(1)}, ...), branch_computations={%region_11.26_spmd, %region_27.36_spmd} | conditional | flops 5637167616 | bytes 133643008 | solution.py:244
  1524.8 63.0 %collective-permute-start.1 = (bf16[197,768]{1,0:T(8,128)(2,1)S(1)}, bf16[197,768]{1,0:T(8,128)(2,1)S(1)}, u32[]{:S(2)}, u32[]{:S(2)}) collective-permute-start(bf16[197,768]{1,0:T(8,128)(2,1)S(1)} %get-tuple-element.771), channel_id=1, source_target_pairs={{8,0},{16,8},{24,16},{9,1},{17,9},{25,17},{10,2},{18,10},{26,18},{... | collective-permute-start | bytes 907784 | tf_op jit(solution)/shard_map/while/body/eval_jaxpr/ppermute | solution.py:17
  1611.9 35.4 %conditional.10 = (f32[197,768]{1,0:T(8,128)}, f32[768,3072]{1,0:T(8,128)}, f32[3072,768]{1,0:T(8,128)}, f32[8,768]{1,0:T(8,128)S(1)}, f32[12,732]{1,0:T(8,128)}) conditional(s32[]{:T(128)} %convert_element_type.186, (f32[197,768]{1,0:T(8,128)S(1)}, f32[8,768]{1,0:T(8,128)S(1)}, bf16[768,3072]{1,0:T(8,128)(2,1)}, f32[197,768]{1,0:T(8,128)S(1)}, ...), branch_computations={%region_11.26_spmd, %region_27.36_spmd} | conditional | flops 5637167616 | bytes 133643008 | solution.py:244
  1648.9 62.4 %collective-permute-start.1 = (bf16[197,768]{1,0:T(8,128)(2,1)S(1)}, bf16[197,768]{1,0:T(8,128)(2,1)S(1)}, u32[]{:S(2)}, u32[]{:S(2)}) collective-permute-start(bf16[197,768]{1,0:T(8,128)(2,1)S(1)} %get-tuple-element.771), channel_id=1, source_target_pairs={{8,0},{16,8},{24,16},{9,1},{17,9},{25,17},{10,2},{18,10},{26,18},{... | collective-permute-start | bytes 907784 | tf_op jit(solution)/shard_map/while/body/eval_jaxpr/ppermute | solution.py:17
  1736.0 35.4 %conditional.10 = (f32[197,768]{1,0:T(8,128)}, f32[768,3072]{1,0:T(8,128)}, f32[3072,768]{1,0:T(8,128)}, f32[8,768]{1,0:T(8,128)S(1)}, f32[12,732]{1,0:T(8,128)}) conditional(s32[]{:T(128)} %convert_element_type.186, (f32[197,768]{1,0:T(8,128)S(1)}, f32[8,768]{1,0:T(8,128)S(1)}, bf16[768,3072]{1,0:T(8,128)(2,1)}, f32[197,768]{1,0:T(8,128)S(1)}, ...), branch_computations={%region_11.26_spmd, %region_27.36_spmd} | conditional | flops 5637167616 | bytes 133643008 | solution.py:244
  1773.0 61.7 %collective-permute-start.1 = (bf16[197,768]{1,0:T(8,128)(2,1)S(1)}, bf16[197,768]{1,0:T(8,128)(2,1)S(1)}, u32[]{:S(2)}, u32[]{:S(2)}) collective-permute-start(bf16[197,768]{1,0:T(8,128)(2,1)S(1)} %get-tuple-element.771), channel_id=1, source_target_pairs={{8,0},{16,8},{24,16},{9,1},{17,9},{25,17},{10,2},{18,10},{26,18},{... | collective-permute-start | bytes 907784 | tf_op jit(solution)/shard_map/while/body/eval_jaxpr/ppermute | solution.py:17
  1861.2 33.3 %all-reduce.1 = (f32[1,8,768]{2,1,0:T(8,128)}, f32[1,12,732]{2,0,1:T(1,128)}) all-reduce(f32[1,8,768]{2,1,0:T(8,128)S(1)} %scatter-add.6, f32[1,12,732]{2,0,1:T(1,128)S(1)} %broadcast_in_dim.101), channel_id=1, replica_groups=mesh['section'=4,'dp'=8] {'dp'}, use_global_device_ids=true, to_apply=%region_41.42 | all-reduce | flops 14928 | bytes 119424 | tf_op jit(solution)/shard_map/psum | solution.py:306
  1894.5 536.7 %all-reduce.5.cloned.1.call-done = (f32[1,768,3072]{2,1,0:T(8,128)}, f32[1,3072,768]{2,1,0:T(8,128)}) async-done(((f32[1,768,3072]{2,1,0:T(8,128)}, f32[1,3072,768]{2,1,0:T(8,128)}), (f32[1,768,3072]{2,1,0:T(8,128)}, f32[1,3072,768]{2,1,0:T(8,128)})) %all-reduce.5.cloned.1.call-update) | async-done | bytes 18874384 | tf_op jit(solution)/shard_map/psum | solution.py:306
  (713 shorter events, 1052.6 us)
Async XLA Ops:
  7.2 2424.1 %all-reduce.5.cloned.1.call-start = ((), (), s32[]{:S(2)}) async-start(), calls=%async_computation | async-start | bytes 37748736 | tf_op jit(solution)/shard_map/psum | solution.py:306
  8.8 150.9 %copy-start.17 = (f32[8,197]{0,1:T(8,128)}, f32[8,197]{0,1:T(8,128)S(1)}, u32[]{:S(2)}) copy-start(f32[8,197]{0,1:T(8,128)S(1)} %copy.60) | copy-start | bytes 18916
  9.7 150.0 %copy-start.19 = (f32[8,197]{0,1:T(8,128)}, f32[8,197]{0,1:T(8,128)S(1)}, u32[]{:S(2)}) copy-start(f32[8,197]{0,1:T(8,128)S(1)} %copy.59) | copy-start | bytes 18916
  184.7 9.4 collective-permute-start
  211.4 9.2 collective-permute-start
  237.9 9.3 collective-permute-start
  264.5 9.2 collective-permute-start
  291.0 9.2 collective-permute-start
  317.6 9.2 collective-permute-start
  344.1 9.2 collective-permute-start
  370.6 9.3 collective-permute-start
  397.2 9.2 collective-permute-start
  423.7 9.2 collective-permute-start
  450.3 9.2 collective-permute-start
  538.2 75.1 %collective-permute-start.1 = (bf16[197,768]{1,0:T(8,128)(2,1)S(1)}, bf16[197,768]{1,0:T(8,128)(2,1)S(1)}, u32[]{:S(2)}, u32[]{:S(2)}) collective-permute-start(bf16[197,768]{1,0:T(8,128)(2,1)S(1)} %get-tuple-element.771), channel_id=1, source_target_pairs={{8,0},{16,8},{24,16},{9,1},{17,9},{25,17},{10,2},{18,10},{26,18},{... | collective-permute-start | bytes 907784 | tf_op jit(solution)/shard_map/while/body/eval_jaxpr/ppermute | solution.py:17
  657.3 79.4 %collective-permute-start.1 = (bf16[197,768]{1,0:T(8,128)(2,1)S(1)}, bf16[197,768]{1,0:T(8,128)(2,1)S(1)}, u32[]{:S(2)}, u32[]{:S(2)}) collective-permute-start(bf16[197,768]{1,0:T(8,128)(2,1)S(1)} %get-tuple-element.771), channel_id=1, source_target_pairs={{8,0},{16,8},{24,16},{9,1},{17,9},{25,17},{10,2},{18,10},{26,18},{... | collective-permute-start | bytes 907784 | tf_op jit(solution)/shard_map/while/body/eval_jaxpr/ppermute | solution.py:17
  780.8 79.5 %collective-permute-start.1 = (bf16[197,768]{1,0:T(8,128)(2,1)S(1)}, bf16[197,768]{1,0:T(8,128)(2,1)S(1)}, u32[]{:S(2)}, u32[]{:S(2)}) collective-permute-start(bf16[197,768]{1,0:T(8,128)(2,1)S(1)} %get-tuple-element.771), channel_id=1, source_target_pairs={{8,0},{16,8},{24,16},{9,1},{17,9},{25,17},{10,2},{18,10},{26,18},{... | collective-permute-start | bytes 907784 | tf_op jit(solution)/shard_map/while/body/eval_jaxpr/ppermute | solution.py:17
  902.7 81.7 %copy-start.30 = (s32[11]{0:T(128)S(1)}, s32[11]{0:T(128)}, u32[]{:S(2)}) copy-start(s32[11]{0:T(128)} %copy-done.29) | copy-start | bytes 136 | tf_op jit(solution)/shard_map/while
  904.3 80.0 %collective-permute-start.1 = (bf16[197,768]{1,0:T(8,128)(2,1)S(1)}, bf16[197,768]{1,0:T(8,128)(2,1)S(1)}, u32[]{:S(2)}, u32[]{:S(2)}) collective-permute-start(bf16[197,768]{1,0:T(8,128)(2,1)S(1)} %get-tuple-element.771), channel_id=1, source_target_pairs={{8,0},{16,8},{24,16},{9,1},{17,9},{25,17},{10,2},{18,10},{26,18},{... | collective-permute-start | bytes 907784 | tf_op jit(solution)/shard_map/while/body/eval_jaxpr/ppermute | solution.py:17
  1026.8 81.7 %copy-start.30 = (s32[11]{0:T(128)S(1)}, s32[11]{0:T(128)}, u32[]{:S(2)}) copy-start(s32[11]{0:T(128)} %copy-done.29) | copy-start | bytes 136 | tf_op jit(solution)/shard_map/while
  1028.4 80.0 %collective-permute-start.1 = (bf16[197,768]{1,0:T(8,128)(2,1)S(1)}, bf16[197,768]{1,0:T(8,128)(2,1)S(1)}, u32[]{:S(2)}, u32[]{:S(2)}) collective-permute-start(bf16[197,768]{1,0:T(8,128)(2,1)S(1)} %get-tuple-element.771), channel_id=1, source_target_pairs={{8,0},{16,8},{24,16},{9,1},{17,9},{25,17},{10,2},{18,10},{26,18},{... | collective-permute-start | bytes 907784 | tf_op jit(solution)/shard_map/while/body/eval_jaxpr/ppermute | solution.py:17
  1150.9 81.7 %copy-start.30 = (s32[11]{0:T(128)S(1)}, s32[11]{0:T(128)}, u32[]{:S(2)}) copy-start(s32[11]{0:T(128)} %copy-done.29) | copy-start | bytes 136 | tf_op jit(solution)/shard_map/while
  1152.5 80.0 %collective-permute-start.1 = (bf16[197,768]{1,0:T(8,128)(2,1)S(1)}, bf16[197,768]{1,0:T(8,128)(2,1)S(1)}, u32[]{:S(2)}, u32[]{:S(2)}) collective-permute-start(bf16[197,768]{1,0:T(8,128)(2,1)S(1)} %get-tuple-element.771), channel_id=1, source_target_pairs={{8,0},{16,8},{24,16},{9,1},{17,9},{25,17},{10,2},{18,10},{26,18},{... | collective-permute-start | bytes 907784 | tf_op jit(solution)/shard_map/while/body/eval_jaxpr/ppermute | solution.py:17
  1276.6 80.0 %collective-permute-start.1 = (bf16[197,768]{1,0:T(8,128)(2,1)S(1)}, bf16[197,768]{1,0:T(8,128)(2,1)S(1)}, u32[]{:S(2)}, u32[]{:S(2)}) collective-permute-start(bf16[197,768]{1,0:T(8,128)(2,1)S(1)} %get-tuple-element.771), channel_id=1, source_target_pairs={{8,0},{16,8},{24,16},{9,1},{17,9},{25,17},{10,2},{18,10},{26,18},{... | collective-permute-start | bytes 907784 | tf_op jit(solution)/shard_map/while/body/eval_jaxpr/ppermute | solution.py:17
  1399.1 81.7 %copy-start.30 = (s32[11]{0:T(128)S(1)}, s32[11]{0:T(128)}, u32[]{:S(2)}) copy-start(s32[11]{0:T(128)} %copy-done.29) | copy-start | bytes 136 | tf_op jit(solution)/shard_map/while
  1400.7 80.0 %collective-permute-start.1 = (bf16[197,768]{1,0:T(8,128)(2,1)S(1)}, bf16[197,768]{1,0:T(8,128)(2,1)S(1)}, u32[]{:S(2)}, u32[]{:S(2)}) collective-permute-start(bf16[197,768]{1,0:T(8,128)(2,1)S(1)} %get-tuple-element.771), channel_id=1, source_target_pairs={{8,0},{16,8},{24,16},{9,1},{17,9},{25,17},{10,2},{18,10},{26,18},{... | collective-permute-start | bytes 907784 | tf_op jit(solution)/shard_map/while/body/eval_jaxpr/ppermute | solution.py:17
  1523.2 81.7 %copy-start.30 = (s32[11]{0:T(128)S(1)}, s32[11]{0:T(128)}, u32[]{:S(2)}) copy-start(s32[11]{0:T(128)} %copy-done.29) | copy-start | bytes 136 | tf_op jit(solution)/shard_map/while
  1524.8 80.0 %collective-permute-start.1 = (bf16[197,768]{1,0:T(8,128)(2,1)S(1)}, bf16[197,768]{1,0:T(8,128)(2,1)S(1)}, u32[]{:S(2)}, u32[]{:S(2)}) collective-permute-start(bf16[197,768]{1,0:T(8,128)(2,1)S(1)} %get-tuple-element.771), channel_id=1, source_target_pairs={{8,0},{16,8},{24,16},{9,1},{17,9},{25,17},{10,2},{18,10},{26,18},{... | collective-permute-start | bytes 907784 | tf_op jit(solution)/shard_map/while/body/eval_jaxpr/ppermute | solution.py:17
  1647.3 81.7 %copy-start.30 = (s32[11]{0:T(128)S(1)}, s32[11]{0:T(128)}, u32[]{:S(2)}) copy-start(s32[11]{0:T(128)} %copy-done.29) | copy-start | bytes 136 | tf_op jit(solution)/shard_map/while
  1648.9 80.0 %collective-permute-start.1 = (bf16[197,768]{1,0:T(8,128)(2,1)S(1)}, bf16[197,768]{1,0:T(8,128)(2,1)S(1)}, u32[]{:S(2)}, u32[]{:S(2)}) collective-permute-start(bf16[197,768]{1,0:T(8,128)(2,1)S(1)} %get-tuple-element.771), channel_id=1, source_target_pairs={{8,0},{16,8},{24,16},{9,1},{17,9},{25,17},{10,2},{18,10},{26,18},{... | collective-permute-start | bytes 907784 | tf_op jit(solution)/shard_map/while/body/eval_jaxpr/ppermute | solution.py:17
  1771.4 81.7 %copy-start.30 = (s32[11]{0:T(128)S(1)}, s32[11]{0:T(128)}, u32[]{:S(2)}) copy-start(s32[11]{0:T(128)} %copy-done.29) | copy-start | bytes 136 | tf_op jit(solution)/shard_map/while
  1773.0 80.0 %collective-permute-start.1 = (bf16[197,768]{1,0:T(8,128)(2,1)S(1)}, bf16[197,768]{1,0:T(8,128)(2,1)S(1)}, u32[]{:S(2)}, u32[]{:S(2)}) collective-permute-start(bf16[197,768]{1,0:T(8,128)(2,1)S(1)} %get-tuple-element.771), channel_id=1, source_target_pairs={{8,0},{16,8},{24,16},{9,1},{17,9},{25,17},{10,2},{18,10},{26,18},{... | collective-permute-start | bytes 907784 | tf_op jit(solution)/shard_map/while/body/eval_jaxpr/ppermute | solution.py:17
  (56 other events, 772.5 us)
Sparse Core Ops, SparseCore 0:
  1853.2 577.9 all-reduce.4
where the time goes:
time: 2470 us; the launch traced here: 2450 us
  starting transfers between devices  766 us (31%)
  waiting for transfers between devices  582 us (24%)
  matrix products  486 us (20%)
  local copies, waits for them, and re-layouts  448 us (18%)
  other arithmetic  80.1 us (3%)
  loops' own time  39.5 us (2%)
  blocking collectives  33.3 us (1%)
    ppermute x22, starting transfers between devices, from_behind(): return lax.ppermute(block, axis, route)  766 us
    psum x1, waiting for transfers between devices, on_device(): summed = lax.psum((grad_matrix, grad_lower, grad_rows, grad_bias), 'dp')  537 us
    dot_general x33, matrix products, matmul(): return jnp.dot(left, right, preferred_element_type=jnp.float32)  217 us
    dot_general x22, matrix products, left_t(): lax.dot_general(left, right, (((0,), (0,)), ((), ())), preferred_element_...  199 us
    dynamic_update_slice x22, local copies, waits for them, and re-layouts, store_at(): lax.dynamic_update_index_in_dim(buffer, jnp.where(valid, update, previous...  144 us
    gather x3, local copies, waits for them, and re-layouts, on_device(): position_bias = rel_bias[:, lookup]  142 us
    dot_general x22, matrix products, right_t(): lax.dot_general(left, right, (((1,), (1,)), ((), ())), preferred_element_...  69.7 us
    dynamic_slice x33, local copies, waits for them, and re-layouts, store_at(): previous = lax.dynamic_index_in_dim(buffer, place, 0, False)  63.1 us
  transfers between devices with their start and end apart: 23, of which 21 were waited for; matrix products, arithmetic and copies ran while one was open for 7% of the time, Pallas kernels for 0%

commit v1 on v0

v1 whole, which is shorter than its diff:
```python
import math
from functools import partial

import jax
import jax.numpy as jnp
from jax import lax
from jax.experimental import pallas as pl
from jax.experimental.pallas import tpu as pltpu
from jax.sharding import PartitionSpec as P

EPS = 1e-06
F32 = jnp.float32
BF = jnp.bfloat16
HD = 64
ANY = pl.BlockSpec(memory_space=pl.ANY)
VMEM = pl.BlockSpec(memory_space=pltpu.VMEM)
SMEM = pl.BlockSpec(memory_space=pltpu.SMEM)


def dot(left, right):
    return jnp.dot(left, right, preferred_element_type=F32)


def dot_nt(left, right):
    return lax.dot_general(left, right, (((1,), (1,)), ((), ())), preferred_element_type=F32)


def dot_tn(left, right):
    return lax.dot_general(left, right, (((0,), (0,)), ((), ())), preferred_element_type=F32)


def norm_stats(x):
    center = x - jnp.mean(x, -1, keepdims=True)
    rstd = lax.rsqrt(jnp.mean(center * center, -1, keepdims=True) + EPS)
    return center * rstd, rstd


def norm_back(g, da, xhat, rstd, gain):
    w = da * gain
    return g + rstd * (w - jnp.mean(w, -1, keepdims=True) - xhat * jnp.mean(w * xhat, -1, keepdims=True))


def rows_sum(v):
    return jnp.sum(v, 0, keepdims=True)


def gelu_parts(h):
    z = jnp.abs(h) * 0.7071067811865476
    t = 1.0 / (1.0 + 0.3275911 * z)
    gauss = jnp.exp(-0.5 * h * h)
    poly = t * (0.127414796 + t * (-0.142248368 + t * (0.7107068705 + t * (-0.7265760135 + t * 0.5307027145))))
    tail = poly * gauss
    phi = jnp.where(h >= 0.0, 1.0 - tail, tail)
    return h * phi, phi + h * (gauss * 0.3989422804014327)


class Copies:
    def __init__(self, sems):
        self.sems, self.used, self.out = sems, 0, []

    def start(self, src, dst):
        copy = pltpu.make_async_copy(src, dst, self.sems.at[self.used])
        self.used += 1
        copy.start()
        return copy

    def choose(self, first, a, b, dst):
        sem = self.sems.at[self.used]
        self.used += 1

        @pl.when(first)
        def _():
            pltpu.make_async_copy(a, dst, sem).start()

        @pl.when(jnp.logical_not(first))
        def _():
            pltpu.make_async_copy(b, dst, sem).start()

        return pltpu.make_async_copy(a, dst, sem)

    def store(self, src, dst):
        self.out.append(self.start(src, dst))

    def store_choose(self, first, src, a, b):
        sem = self.sems.at[self.used]
        self.used += 1

        @pl.when(first)
        def _():
            pltpu.make_async_copy(src, a, sem).start()

        @pl.when(jnp.logical_not(first))
        def _():
            pltpu.make_async_copy(src, b, sem).start()

        self.out.append(pltpu.make_async_copy(src, a, sem))

    def finish(self):
        for copy in self.out:
            copy.wait()


def image_of(ref, i):
    return ref.at[i] if len(ref.shape) == 3 else ref


def head_masks(scale):
    lane = lax.broadcasted_iota(jnp.int32, (1, 2 * HD), 1)
    low = jnp.where(lane < HD, scale, 0.0).astype(BF)
    high = jnp.where(lane < HD, 0.0, scale).astype(BF)
    return low, high


def attend_forward(i, refs_in, refs_state, refs_extra, scratch):
    flags, x_ref, vec_ref, own_ref, other_ref, bias_ref = refs_in
    x_ref = image_of(x_ref, i)
    sa, a1, ctx, y1, pb = refs_state
    x_v, w_v, bias_v, a_v, qkv_v, pb_v, c_v, b_v, y_v, sems = scratch
    rows, width = x_v.shape
    heads, keys = pb_v.shape[0], pb_v.shape[2]

    @pl.when(flags[0] == 1)
    def _():
        cp = Copies(sems)
        first = flags[1] == 0
        in_x = cp.start(x_ref, x_v)
        three = pl.ds(0, 3 * width)
        last = pl.ds(3 * width, width)
        in_w = cp.choose(first, own_ref.at[:, three], other_ref.at[:, three], w_v.at[:, three])
        in_b = cp.start(bias_ref, bias_v)
        in_p = cp.choose(first, own_ref.at[:, last], other_ref.at[:, last], w_v.at[:, last])
        in_x.wait()
        cp.store(x_v, sa.at[i, 0])
        x = x_v[...].astype(F32)
        xhat, rstd = norm_stats(x)
        a_v[...] = (xhat * vec_ref[0:1, :] + vec_ref[1:2, :]).astype(BF)
        cp.store(a_v, a1.at[i])
        qkv_v[rows:, :] = jnp.zeros((keys - rows, 3 * width), BF)
        in_w.wait()
        a = a_v[...]
        block = 256
        for j in range(3 * width // block):
            cols = slice(j * block, (j + 1) * block)
            part = dot(a, w_v[:, cols])
            kind, at = divmod(j * block, width)
            if kind == 0:
                part = part + vec_ref[4:5, at : at + block]
            if kind == 2:
                part = part + vec_ref[5:6, at : at + block]
            qkv_v[0:rows, cols] = part.astype(BF)
        for kind in range(3):
            cp.store(qkv_v.at[0:rows, pl.ds(kind * width, width)], sa.at[i, 1 + kind])
        in_b.wait()
        scaled = head_masks(HD ** (-0.5))
        plain = head_masks(1.0)
        for j in range(heads // 2):
            q = qkv_v[0:rows, j * 128 : (j + 1) * 128]
            k = qkv_v[:, width + j * 128 : width + (j + 1) * 128]
            u = qkv_v[:, 2 * width + j * 128 : 2 * width + (j + 1) * 128]
            total = None
            for t in range(2):
                s = dot_nt(q * scaled[t], k) + bias_v[2 * j + t]
                e = jnp.exp(s - jnp.max(s, -1, keepdims=True))
                p = (e * (1.0 / jnp.sum(e, -1, keepdims=True))).astype(BF)
                pb_v[2 * j + t] = p
                part = dot(p, u * plain[t])
                total = part if total is None else total + part
            c_v[:, j * 128 : (j + 1) * 128] = total.astype(BF)
        cp.store(pb_v, pb.at[i])
        cp.store(c_v, ctx.at[i])
        in_p.wait()
        b = dot(c_v[...], w_v[:, 3 * width :]) + vec_ref[3:4, :]
        b_v[...] = b.astype(BF)
        cp.store(b_v, sa.at[i, 4])
        y_v[...] = (x_v[...].astype(F32) + vec_ref[2:3, :] * b).astype(BF)
        cp.store(y_v, y1.at[i])
        cp.finish()


def feed_forward(i, refs_in, refs_state, refs_extra, scratch):
    flags, y1, vec_ref, own_ref, other_ref, own_d, other_d = refs_in
    lh0, lh1, rh0, rh1, gp, b2, y2, dx1, vgf = refs_state
    (send,) = refs_extra
    x_v, w1_v, w2_v, a_v, g_v, gp_v, b_v, y_v, sems = scratch
    rows, width = x_v.shape
    hidden = g_v.shape[1]
    cuts = 4
    step = hidden // cuts

    @pl.when(flags[0] == 1)
    def _():
        cp = Copies(sems)
        first = flags[1] == 0
        in_x = cp.start(y1.at[i], x_v)
        in_1 = []
        for c in range(cuts):
            at = pl.ds(c * step, step)
            in_1.append(cp.choose(first, other_ref.at[:, at], own_ref.at[:, at], w1_v.at[:, at]))
        in_2 = cp.choose(first, other_d, own_d, w2_v)
        in_x.wait()
        xhat, rstd = norm_stats(x_v[...].astype(F32))
        a_v[...] = (xhat * vec_ref[0:1, :] + vec_ref[1:2, :]).astype(BF)
        cp.store_choose(first, a_v, rh1.at[i], rh0.at[i])
        a = a_v[...]
        block = 256
        for j in range(hidden // block):
            if j * block % step == 0:
                in_1[j * block // step].wait()
            row, at = divmod(j * block, width)
            cols = slice(j * block, (j + 1) * block)
            h = dot(a, w1_v[:, cols]) + vec_ref[4 + row : 5 + row, at : at + block]
            value, slope = gelu_parts(h)
            g_v[:, cols] = value.astype(BF)
            gp_v[:, cols] = slope.astype(BF)
        cp.store_choose(first, g_v, lh0.at[i], lh1.at[i])
        cp.store(gp_v, gp.at[i])
        in_2.wait()
        b = dot(g_v[...], w2_v[...]) + vec_ref[3:4, :]
        b_v[...] = b.astype(BF)
        y_v[...] = (x_v[...].astype(F32) + vec_ref[2:3, :] * b).astype(BF)
        cp.store(y_v, send)
        cp.store(b_v, b2.at[i])
        cp.store(y_v, y2.at[i])
        cp.finish()


def feed_backward(i, refs_in, refs_state, refs_extra, scratch):
    flags, g_ref, vec_ref, own_ref, other_ref, own_d, other_d, y1 = refs_in
    lh0, lh1, rh0, rh1, gp, b2, y2, dx1, vgf = refs_state
    g_ref = image_of(g_ref, i)
    x_v, gin_v, w1_v, w2_v, gp_v, b_v, e_v, dh_v, dx_v, vg_v, sems = scratch
    rows, width = x_v.shape
    hidden = dh_v.shape[1]
    cuts = 4
    step = hidden // cuts

    @pl.when(flags[0] == 1)
    def _():
        cp = Copies(sems)
        first = flags[1] == 0
        in_g = cp.start(g_ref, gin_v)
        in_2 = []
        for c in range(cuts):
            at = pl.ds(c * step, step)
            in_2.append(cp.choose(first, other_d.at[at], own_d.at[at], w2_v.at[at]))
        in_p = cp.start(gp.at[i], gp_v)
        in_b = cp.start(b2.at[i], b_v)
        in_x = cp.start(y1.at[i], x_v)
        in_1 = cp.choose(first, other_ref, own_ref, w1_v)
        in_g.wait()
        g = gin_v[...].astype(F32)
        scaled = g * vec_ref[2:3, :]
        e_v[...] = scaled.astype(BF)
        cp.store_choose(first, e_v, rh0.at[i], rh1.at[i])
        vg_v[3:4, :] = rows_sum(scaled)
        in_p.wait()
        e = e_v[...]
        block = 256
        for j in range(hidden // block):
            if j * block % step == 0:
                in_2[j * block // step].wait()
            row, at = divmod(j * block, width)
            cols = slice(j * block, (j + 1) * block)
            dh = dot_nt(e, w2_v[cols, :]) * gp_v[:, cols].astype(F32)
            dh_v[:, cols] = dh.astype(BF)
            vg_v[4 + row : 5 + row, at : at + block] = rows_sum(dh)
        cp.store_choose(first, dh_v, lh1.at[i], lh0.at[i])
        in_b.wait()
        vg_v[2:3, :] = rows_sum(gin_v[...].astype(F32) * b_v[...].astype(F32))
        in_x.wait()
        in_1.wait()
        da = dot_nt(dh_v[...], w1_v[...])
        xhat, rstd = norm_stats(x_v[...].astype(F32))
        vg_v[0:1, :] = rows_sum(da * xhat)
        vg_v[1:2, :] = rows_sum(da)
        dx = norm_back(gin_v[...].astype(F32), da, xhat, rstd, vec_ref[0:1, :])
        dx_v[...] = dx.astype(BF)
        cp.store(dx_v, dx1.at[i])
        cp.store(vg_v, vgf.at[i])
        cp.finish()


def attend_backward(i, refs_in, refs_state, refs_extra, scratch):
    flags, dx1, vec_ref, own_ref, other_ref, sa, pb = refs_in
    ea, dq, dl, dx0, vga = refs_state
    (send,) = refs_extra
    x_v, gin_v, w_v, pb_v, b_v, e_v, qkv_v, dc_v, dq_v, dl_v, dx_v, vg_v, sems = scratch
    rows, width = x_v.shape
    heads, keys = pb_v.shape[0], pb_v.shape[2]

    @pl.when(flags[0] == 1)
    def _():
        cp = Copies(sems)
        first = flags[1] == 0
        three = pl.ds(0, 3 * width)
        last = pl.ds(3 * width, width)
        in_g = cp.start(dx1.at[i], gin_v)
        in_p = cp.choose(first, own_ref.at[:, last], other_ref.at[:, last], w_v.at[:, last])
        ins = [cp.start(sa.at[i, 1 + kind], qkv_v.at[0:rows, pl.ds(kind * width, width)]) for kind in range(3)]
        in_pb = cp.start(pb.at[i], pb_v)
        in_b = cp.start(sa.at[i, 4], b_v)
        in_x = cp.start(sa.at[i, 0], x_v)
        in_w = cp.choose(first, own_ref.at[:, three], other_ref.at[:, three], w_v.at[:, three])
        qkv_v[rows:, :] = jnp.zeros((keys - rows, 3 * width), BF)
        in_g.wait()
        scaled = gin_v[...].astype(F32) * vec_ref[2:3, :]
        e_v[...] = scaled.astype(BF)
        cp.store(e_v, ea.at[i])
        vg_v[3:4, :] = rows_sum(scaled)
        vg_v[6:8, :] = jnp.zeros((2, width), F32)
        in_p.wait()
        dc_v[...] = dot_nt(e_v[...], w_v[:, 3 * width :]).astype(BF)
        for copy in ins:
            copy.wait()
        in_pb.wait()
        factor = HD ** (-0.5)
        plain = head_masks(1.0)
        for j in range(heads // 2):
            cols = slice(j * 128, (j + 1) * 128)
            q = qkv_v[0:rows, j * 128 : (j + 1) * 128]
            k = qkv_v[:, width + j * 128 : width + (j + 1) * 128]
            u = qkv_v[:, 2 * width + j * 128 : 2 * width + (j + 1) * 128]
            dc = dc_v[:, cols]
            dq_t, dk_t, du_t = None, None, None
            for t in range(2):
                dc_t = dc * plain[t]
                p = pb_v[2 * j + t]
                dp = dot_nt(dc_t, u)
                pf = p.astype(F32)
                wp = pf * dp
                ds = wp - pf * jnp.sum(wp, -1, keepdims=True)
                dlog = (ds * factor).astype(BF)
                dl_v[2 * j + t] = dlog
                du = dot_tn(p, dc_t)
                dqp = dot(dlog, k * plain[t])
                dkp = dot_tn(dlog, q * plain[t])
                dq_t = dqp if dq_t is None else dq_t + dqp
                dk_t = dkp if dk_t is None else dk_t + dkp
                du_t = du if du_t is None else du_t + du
            dq_v[:, j * 128 : (j + 1) * 128] = dq_t.astype(BF)
            dq_v[:, width + j * 128 : width + (j + 1) * 128] = dk_t[0:rows].astype(BF)
            dq_v[:, 2 * width + j * 128 : 2 * width + (j + 1) * 128] = du_t[0:rows].astype(BF)
            vg_v[4:5, cols] = rows_sum(dq_t)
            vg_v[5:6, cols] = rows_sum(du_t)
        cp.store(dl_v, dl.at[i])
        cp.store(dq_v, dq.at[i])
        in_b.wait()
        vg_v[2:3, :] = rows_sum(gin_v[...].astype(F32) * b_v[...].astype(F32))
        in_x.wait()
        in_w.wait()
        da = dot_nt(dq_v[...], w_v[:, 0 : 3 * width])
        xhat, rstd = norm_stats(x_v[...].astype(F32))
        vg_v[0:1, :] = rows_sum(da * xhat)
        vg_v[1:2, :] = rows_sum(da)
        dx = norm_back(gin_v[...].astype(F32), da, xhat, rstd, vec_ref[0:1, :])
        dx_v[...] = dx.astype(BF)
        cp.store(dx_v, send)
        cp.store(dx_v, dx0.at[i])
        cp.store(vg_v, vga.at[i])
        cp.finish()


def run(body, i, name, ins, specs, state, shapes, extra, scratch, sems, flops, moved):
    fresh = state is None
    n_in, n_state, n_extra = len(ins), len(shapes), len(extra)
    given = 0 if fresh else n_state

    def kernel(*refs):
        refs_in = refs[:n_in]
        outs = refs[n_in + given : n_in + given + n_state]
        more = refs[n_in + given + n_state : n_in + given + n_state + n_extra]
        body(i, refs_in, outs, more, refs[n_in + given + n_state + n_extra :])

    made = pl.pallas_call(
        kernel,
        out_shape=tuple(shapes) + tuple(extra),
        in_specs=list(specs) + [ANY] * given,
        out_specs=tuple([ANY] * (n_state + n_extra)),
        scratch_shapes=[pltpu.VMEM(s.shape, s.dtype) for s in scratch] + [pltpu.SemaphoreType.DMA((sems,))],
        input_output_aliases={} if fresh else {n_in + k: k for k in range(n_state)},
        compiler_params=pltpu.CompilerParams(vmem_limit_bytes=56 * 2**20),
        cost_estimate=pl.CostEstimate(flops=flops, bytes_accessed=moved, transcendentals=0),
        name=name,
    )(*ins, *([] if fresh else state))
    return list(made[:n_state]), list(made[n_state:])


def sd(shape, dtype=BF):
    return jax.ShapeDtypeStruct(shape, dtype)


class Kernels:
    def __init__(self, images, rows, keys, width, hidden, heads):
        self.n, self.r, self.k, self.d, self.f, self.h = images, rows, keys, width, hidden, heads

    def att_f(self, i, flags, x, vec, own, other, bias, state):
        n, r, k, d, h = self.n, self.r, self.k, self.d, self.h
        shapes = [sd((n, 5, r, d)), sd((n, r, d)), sd((n, r, d)), sd((n, r, d)), sd((n, h, r, k))]
        scratch = [sd((r, d)), sd((d, 4 * d)), sd((h, r, k), F32), sd((r, d)), sd((k, 3 * d)), sd((h, r, k)), sd((r, d)), sd((r, d)), sd((r, d))]
        return run(attend_forward, i, "attend_forward", [flags, x, vec, own, other, bias], [SMEM, ANY, VMEM, ANY, ANY, ANY], state, shapes, [], scratch, 16, 2 * r * d * 4 * d + 4 * h * r * k * HD, 12000000)

    def feed_state(self):
        n, r, d, f = self.n, self.r, self.d, self.f
        wide, narrow = sd((n, r, f)), sd((n, r, d))
        return [wide, wide, narrow, narrow, wide, narrow, narrow, narrow, sd((n, 8, d), F32)]

    def ff_f(self, i, flags, y1, vec, own, other, own_d, other_d, state):
        r, d, f = self.r, self.d, self.f
        scratch = [sd((r, d)), sd((d, f)), sd((f, d)), sd((r, d)), sd((r, f)), sd((r, f)), sd((r, d)), sd((r, d))]
        return run(feed_forward, i, "feed_forward", [flags, y1, vec, own, other, own_d, other_d], [SMEM, ANY, VMEM, ANY, ANY, ANY, ANY], state, self.feed_state(), [sd((r, d))], scratch, 16, 4 * r * d * f, 12000000)

    def ff_b(self, i, flags, g, vec, own, other, own_d, other_d, y1, state):
        r, d, f = self.r, self.d, self.f
        scratch = [sd((r, d)), sd((r, d)), sd((d, f)), sd((f, d)), sd((r, f)), sd((r, d)), sd((r, d)), sd((r, f)), sd((r, d)), sd((8, d), F32)]
        return run(feed_backward, i, "feed_backward", [flags, g, vec, own, other, own_d, other_d, y1], [SMEM, ANY, VMEM] + [ANY] * 5, state, self.feed_state(), [], scratch, 16, 4 * r * d * f, 12000000)

    def att_b(self, i, flags, dx1, vec, own, other, sa, pb, state):
        n, r, k, d, h = self.n, self.r, self.k, self.d, self.h
        shapes = [sd((n, r, d)), sd((n, r, 3 * d)), sd((n, h, r, k)), sd((n, r, d)), sd((n, 8, d), F32)]
        scratch = [sd((r, d)), sd((r, d)), sd((d, 4 * d)), sd((h, r, k)), sd((r, d)), sd((r, d)), sd((k, 3 * d)), sd((r, d)), sd((r, 3 * d)), sd((h, r, k)), sd((r, d)), sd((8, d), F32)]
        return run(attend_backward, i, "attend_backward", [flags, dx1, vec, own, other, sa, pb], [SMEM, ANY, VMEM] + [ANY] * 4, state, shapes, [sd((r, d))], scratch, 20, 2 * r * d * 4 * d + 8 * h * r * k * HD, 12000000)


def swap(block, pairs):
    return lax.ppermute(block, "section", pairs)


def bias_rows(table, grid, rows, keys):
    heads = table.shape[0]
    side = 2 * grid - 1
    flipped = table[:, : side * side].reshape(heads, side, side)[:, ::-1, ::-1]
    by_col = jnp.stack([flipped[:, :, grid - 1 - c : side - c] for c in range(grid)], 1)
    by_col = by_col.reshape(heads, grid, side * grid)
    patches = grid * grid
    block = jnp.concatenate(
        [by_col[:, :, grid * (grid - 1 - r) : grid * (grid - 1 - r) + patches] for r in range(grid)], 1
    )
    upper = jnp.broadcast_to(table[:, side * side][:, None, None], (heads, 1, patches))
    left = jnp.broadcast_to(table[:, side * side + 1][:, None, None], (heads, patches, 1))
    corner = table[:, side * side + 2][:, None, None]
    full = jnp.concatenate([jnp.concatenate([corner, upper], 2), jnp.concatenate([left, block], 2)], 1)
    full = jnp.pad(full, ((0, 0), (0, rows - patches - 1), (0, 0)))
    return jnp.pad(full, ((0, 0), (0, 0), (0, keys - patches - 1)), constant_values=-1e30)


def table_sums(grad, grid):
    heads = grad.shape[0]
    side, patches = 2 * grid - 1, grid * grid
    block = grad[:, 1:, 1:]
    wide = side * grid
    by_col = 0.0
    for r in range(grid):
        at = grid * (grid - 1 - r)
        by_col = by_col + jnp.pad(block[:, r * grid : (r + 1) * grid], ((0, 0), (0, 0), (at, wide - at - patches)))
    by_col = by_col.reshape(heads, grid, side, grid)
    flipped = 0.0
    for c in range(grid):
        at = grid - 1 - c
        flipped = flipped + jnp.pad(by_col[:, c], ((0, 0), (0, 0), (at, side - at - grid)))
    inner = flipped[:, ::-1, ::-1].reshape(heads, side * side)
    tail = jnp.stack([jnp.sum(grad[:, 0, 1:], 1), jnp.sum(grad[:, 1:, 0], 1), grad[:, 0, 0]], 1)
    return jnp.concatenate([inner, tail], 1)


def ring_sum(jobs, axis):
    n = lax.axis_size(axis)
    if n > 16 or n % 2:
        return [
            lax.psum((own.astype(F32) + other.astype(F32)).astype(BF), axis) for own, other, streams in jobs
        ]
    order = list(range(0, n, 2)) + list(range(n - 1, 0, -2))
    place = [0] * n
    for k, device in enumerate(order):
        place[device] = k
    at = jnp.array(place, jnp.int32)[lax.axis_index(axis)]
    route = {
        1: [(order[k], order[(k + 1) % n]) for k in range(n)],
        -1: [(order[k], order[(k - 1) % n]) for k in range(n)],
    }
    lanes = []
    totals = []
    for number, (own, other, streams) in enumerate(jobs):
        tall, wide = own.shape[0] // n, own.shape[1] // streams
        totals.append(jnp.zeros(own.shape, BF))
        for s in range(streams):
            lanes.append((number, own, other, tall, wide, s, 1 if s % 2 == 0 else -1))

    def take(lane, chunk):
        number, own, other, tall, wide, s, way = lane
        corner = ((chunk % n) * tall, s * wide)
        left = lax.dynamic_slice(own, corner, (tall, wide)).astype(F32)
        return left + lax.dynamic_slice(other, corner, (tall, wide)).astype(F32)

    def put(lane, chunk, value):
        number, own, other, tall, wide, s, way = lane
        totals[number] = lax.dynamic_update_slice(totals[number], value, ((chunk % n) * tall, s * wide))

    held = [take(lane, at).astype(BF) for lane in lanes]
    for k in range(n - 1):
        for m, lane in enumerate(lanes):
            got = lax.ppermute(held[m], axis, route[lane[6]])
            held[m] = (got.astype(F32) + take(lane, at - lane[6] * (k + 1))).astype(BF)
    for m, lane in enumerate(lanes):
        put(lane, at + lane[6], held[m])
    for k in range(n - 1):
        for m, lane in enumerate(lanes):
            held[m] = lax.ppermute(held[m], axis, route[lane[6]])
            put(lane, at - lane[6] * k, held[m])
    return totals


def on_device(embeds, mask, cotangent, section_weight, down_weight, section_vectors, rel_table):
    sections = lax.axis_size("section")
    now = lax.axis_index("section")
    core, stage = now % 2, now // 2
    images, length, width = embeds.shape
    half = images // 2
    hidden = section_weight.shape[2]
    heads = rel_table.shape[1]
    rows, keys = -(-length // 16) * 16, -(-length // 128) * 128
    grid = math.isqrt(length - 1)
    both = [(s, s ^ 1) for s in range(sections)]
    to_low = [(s, s - 1) for s in range(1, sections, 2)]
    to_high = [(s, s + 1) for s in range(0, sections, 2)]
    onward = [(s, s + 2) for s in range(sections - 2)]
    back = [(s + 2, s) for s in range(sections - 2)]
    low = core == 0

    own_w, own_d, own_v, own_t = section_weight[0], down_weight[0], section_vectors[0], rel_table[0]
    other_v = swap(own_v, both)
    table = jnp.where(low, own_t, swap(own_t, to_high))
    other_w = swap(own_w, both)
    other_d = swap(own_d, to_low)
    vec_a, vec_f = jnp.where(low, own_v, other_v), jnp.where(low, other_v, own_v)
    bias = bias_rows(table, grid, rows, keys)

    def mine_of(block):
        return lax.dynamic_slice_in_dim(block, core * half, half, 0)

    cover = mine_of(mask)[:, :, None] == 1
    start = jnp.where(cover, vec_a[6].astype(BF), mine_of(embeds))
    pad = ((0, 0), (0, rows - length), (0, 0))
    start = jnp.pad(start, pad)
    upstream = jnp.pad(mine_of(cotangent), pad)

    kern = Kernels(half, rows, keys, width, hidden, heads)
    flags_a = jnp.stack([(stage == 0).astype(jnp.int32), core])
    flags_b = jnp.stack([(stage == 1).astype(jnp.int32), core])
    att, feed = None, None

    def forward(i, flags, x):
        nonlocal att, feed
        att, _ = kern.att_f(i, flags, x, vec_a, own_w, other_w, bias, att)
        feed, (send,) = kern.ff_f(i, flags, att[3], vec_f, own_w, other_w, own_d, other_d, feed)
        return send

    arrived = [swap(forward(i, flags_a, start), onward) for i in range(half)]
    for i in range(half):
        forward(i, flags_b, arrived[i])

    grads = None

    def backward(i, flags, g):
        nonlocal feed, grads
        feed, _ = kern.ff_b(i, flags, g, vec_f, own_w, other_w, own_d, other_d, att[3], feed)
        grads, (send,) = kern.att_b(i, flags, feed[7], vec_a, own_w, other_w, att[0], att[4], grads)
        return send

    returned = [swap(backward(i, flags_b, upstream), back) for i in range(half)]
    for i in range(half):
        backward(i, flags_a, returned[i])

    sa, a1, ctx, y1, pb = att
    lh0, lh1, rh0, rh1, gp, b2, y2, dx1, vgf = feed
    ea, dq, dl, dx0, vga = grads

    def flat(block):
        return block.reshape(half * rows, block.shape[2])

    sent_f = dot_tn(flat(rh0), flat(lh0)).astype(BF)
    got_f = swap(sent_f, both)
    own_f = dot_tn(flat(rh1), flat(lh1)).astype(BF)

    part = width // 2

    def att_part(which):
        left = lax.dynamic_slice_in_dim(flat(a1), which * part, part, 1)
        right = lax.dynamic_slice_in_dim(flat(ctx), which * part, part, 1)
        return jnp.concatenate([dot_tn(left, flat(dq)).astype(BF), dot_tn(right, flat(ea)).astype(BF)], 1)

    got_a = swap(att_part(1 - core), both)
    own_a = att_part(core)
    sum_f, sum_a = ring_sum([(own_f, got_f, 4), (own_a, got_a, 4)], "dp")

    from_f = swap(sum_f, to_high)
    from_a = swap(sum_a, to_low)
    grad_weight = jnp.where(low, jnp.concatenate([sum_a, from_a], 0), from_f).astype(F32)
    grad_down = jnp.where(low, 0.0, sum_f.astype(F32)).T

    rows_a = jnp.sum(vga, 0)
    token = jnp.sum(jnp.where(cover, dx0[:, :length].astype(F32), 0.0), (0, 1))
    rows_a = rows_a.at[6].add(jnp.where(stage == 0, token, 0.0))
    rows_f = jnp.sum(vgf, 0)
    rows_sum_ = jnp.where(low, rows_a, rows_f) + swap(jnp.where(low, rows_f, rows_a), both)
    scores = jnp.sum(dl[:, :, :length, :length].astype(F32), 0)
    sums = table_sums(scores, grid) * (HD ** 0.5)
    sums = jnp.where(low, sums + swap(sums, to_low), 0.0)
    grad_rows, grad_table = lax.psum((rows_sum_, sums), "dp")

    def gather_images(a_part, f_part):
        mine, theirs = jnp.where(low, a_part, f_part), jnp.where(low, f_part, a_part)
        got = swap(theirs, both)
        return jnp.concatenate([jnp.where(low, mine, got), jnp.where(low, got, mine)], 0)[:, :length]

    activations = gather_images(y1, y2)
    input_grads = gather_images(dx0, dx1).astype(F32)
    hide = (mask[:, :, None] == 1) & (now == 0)
    input_grads = jnp.where(hide, 0.0, input_grads)
    return (
        activations[None],
        input_grads[None],
        grad_weight[None],
        grad_down[None],
        grad_rows[None],
        grad_table[None],
    )


def solution(mesh):
    placed = (
        P("dp", None, None),
        P("dp", None),
        P("dp", None, None),
        P("section", None, None),
        P("section", None, None),
        P("section", None, None),
        P("section", None, None),
    )
    return jax.shard_map(
        on_device,
        mesh=mesh,
        in_specs=placed,
        out_specs=(
            P("section", "dp", None, None),
            P("section", "dp", None, None),
            P("section", None, None),
            P("section", None, None),
            P("section", None, None),
            P("section", None, None),
        ),
        check_vma=False,
    )
```

time: 2470 us -> 745 us (0.30)
  the two profiles are of different devices: /device:TPU:1 before, /device:TPU:0 now
where the time goes in v1:
time: 745 us; the launch traced here: 733 us
  Pallas kernels  180 us (24%)
  waiting for transfers between devices  160 us (21%)
  starting transfers between devices  129 us (17%)
  local copies, waits for them, and re-layouts  107 us (14%)
  other arithmetic  82.5 us (11%)
  blocking collectives  34.2 us (5%)
  matrix products  26.7 us (4%)
  between operations  13.6 us (2%)
    pallas_call x32, Pallas kernels, run(): pl.pallas_call(kernel, out_shape=tuple(shapes) + tuple(extra), in_specs=l...  180 us
    ppermute x56, waiting for transfers between devices, ring_sum(): held[m] = lax.ppermute(held[m], axis, route[lane[6]])  89.8 us
    ppermute x56, waiting for transfers between devices, ring_sum(): got = lax.ppermute(held[m], axis, route[lane[6]])  60.1 us
    ppermute x56, starting transfers between devices, ring_sum(): got = lax.ppermute(held[m], axis, route[lane[6]])  57.3 us
    ppermute x56, starting transfers between devices, ring_sum(): held[m] = lax.ppermute(held[m], axis, route[lane[6]])  47.5 us
    dynamic_update_slice x56, local copies, waits for them, and re-layouts, put(): lax.dynamic_update_slice(totals[number], value, (chunk % n * tall, s * wi...  37.2 us
    psum x1, blocking collectives, on_device(): grad_rows, grad_table = lax.psum((rows_sum_, sums), 'dp')  34.2 us
    convert_element_type x27, other arithmetic, ring_sum(): held[m] = (got.astype(F32) + take(lane, at - lane[6] * (k + 1))).astype(BF)  32.1 us
  transfers between devices with their start and end apart: 132, of which 69 were waited for; matrix products, arithmetic and copies ran while one was open for 25% of the time, Pallas kernels for 19%

profile of v1, /device:TPU:0, one launch (start us, length us, event | category | flops | bytes accessed | tf_op | source)
XLA Modules:
  0.0 732.6 jit_solution(18013658302439460031)
XLA Ops:
  3.2 5.1 collective-permute-start.2
  9.8 4.7 constant_dynamic-slice_fusion
  28.4 15.4 %concatenate.34 = f32[12,196,196]{2,1,0:T(8,128)S(1)} concatenate(f32[12,14,196]{2,1,0:T(8,128)} %get-tuple-element.605, f32[12,14,196]{2,1,0:T(8,128)} %get-tuple-element.604, f32[12,14,196]{2,1,0:T(8,128)} %get-tuple-element.603, f32[12,14,196]{2,1,0:T(8,128)} %get-tuple-element.602, f32[12,14,196]{2,1,0:T(8,128)} %get-tuple-element.601, f32[12,14,196]{2,1,0:T(8,128)} %get-tuple-element.600, ...), dimensions={1} | concatenate | bytes 3687936 | tf_op jit(solution)/shard_map/concatenate | solution.py:435
  46.4 8.3 %attend_forward.8 = (bf16[4,5,208,768]{3,2,1,0:T(8,128)(2,1)}, bf16[4,208,768]{2,1,0:T(8,128)(2,1)}, bf16[4,208,768]{2,1,0:T(8,128)(2,1)}, bf16[4,208,768]{2,1,0:T(8,128)(2,1)}, bf16[4,12,208,256]{3,2,1,0:T(8,128)(2,1)}) custom-call(s32[2]{0:T(128)} %pad_add_fusion.3.refs_0_, bf16[4,208,768]{2,1,0:T(8,128)(2,1)} %pad.129.refs_1_, f32[8,768]{1,0:T(8,128)} %copy-done.21, ...), custom_call_target="tpu_custom_call" | custom-call | flops 1145044992 | bytes 12000000 | tf_op jit(solution)/shard_map/attend_forward/pallas_call | solution.py:374
  54.8 8.4 %feed_forward.8 = (bf16[4,208,3072]{2,1,0:T(8,128)(2,1)}, bf16[4,208,3072]{2,1,0:T(8,128)(2,1)}, bf16[4,208,768]{2,1,0:T(8,128)(2,1)}, bf16[4,208,768]{2,1,0:T(8...) custom-call(s32[2]{0:T(128)} %pad_add_fusion.3.refs_0_, ...), custom_call_target="tpu_custom_call" | custom-call | flops 1962934272 | bytes 12000000 | tf_op jit(solution)/shard_map/feed_forward/pallas_call | solution.py:374
  64.5 8.1 %attend_forward.9 = (bf16[4,5,208,768]{3,2,1,0:T(8,128)(2,1)}, bf16[4,208,768]{2,1,0:T(8,128)(2,1)}, bf16[4,208,768]{2,1,0:T(8,128)(2,1)}, bf16[4,208,768]{2,1,0:T(8,128)(2,1)}, bf16[4,12,208,256]{3,2,1,0:T(8,128)(2,1)}) custom-call(s32[2]{0:T(128)} %pad_add_fusion.3.refs_0_, ...), custom_call_target="tpu_custom_call", output_to_operand_aliasing={{0}: (6, {}), {1}: (7, {}), {2}: (8, {}), {3}: (9, {}), {4}... | custom-call | flops 1145044992 | bytes 12000000 | tf_op jit(solution)/shard_map/attend_forward/pallas_call | solution.py:374
  72.7 8.8 %feed_forward.9 = (bf16[4,208,3072]{2,1,0:T(8,128)(2,1)}, bf16[4,208,3072]{2,1,0:T(8,128)(2,1)}, bf16[4,208,768]{2,1,0:T(8,128)(2,1)}, bf16[4,208,768]{2,1,0:T(8...) custom-call(s32[2]{0:T(128)} %pad_add_fusion.3.refs_0_, ...), custom_call_target="tpu_custom_call", output_to_operand_aliasing={{0}: (7, {}), {1}: (8, {}), {2}: (9, {}), {3}: (10, {}), {4... | custom-call | flops 1962934272 | bytes 12000000 | tf_op jit(solution)/shard_map/feed_forward/pallas_call | solution.py:374
  82.8 8.1 %attend_forward.10 = (bf16[4,5,208,768]{3,2,1,0:T(8,128)(2,1)}, bf16[4,208,768]{2,1,0:T(8,128)(2,1)}, bf16[4,208,768]{2,1,0:T(8,128)(2,1)}, bf16[4,208,768]{2,1,0:T(8,128)(2,1)}, bf16[4,12,208,256]{3,2,1,0:T(8,128)(2,1)}) custom-call(s32[2]{0:T(128)} %pad_add_fusion.3.refs_0_, ...), custom_call_target="tpu_custom_call", output_to_operand_aliasing={{0}: (6, {}), {1}: (7, {}), {2}: (8, {}), {3}: (9, {}), {4}... | custom-call | flops 1145044992 | bytes 12000000 | tf_op jit(solution)/shard_map/attend_forward/pallas_call | solution.py:374
  91.0 8.6 %feed_forward.10 = (bf16[4,208,3072]{2,1,0:T(8,128)(2,1)}, bf16[4,208,3072]{2,1,0:T(8,128)(2,1)}, bf16[4,208,768]{2,1,0:T(8,128)(2,1)}, bf16[4,208,768]{2,1,0:T(...) custom-call(s32[2]{0:T(128)} %pad_add_fusion.3.refs_0_, ...), custom_call_target="tpu_custom_call", output_to_operand_aliasing={{0}: (7, {}), {1}: (8, {}), {2}: (9, {}), {3}: (10, {}), {4... | custom-call | flops 1962934272 | bytes 12000000 | tf_op jit(solution)/shard_map/feed_forward/pallas_call | solution.py:374
  100.9 8.1 %attend_forward.11 = (bf16[4,5,208,768]{3,2,1,0:T(8,128)(2,1)}, bf16[4,208,768]{2,1,0:T(8,128)(2,1)}, bf16[4,208,768]{2,1,0:T(8,128)(2,1)}, bf16[4,208,768]{2,1,0:T(8,128)(2,1)}, bf16[4,12,208,256]{3,2,1,0:T(8,128)(2,1)}) custom-call(s32[2]{0:T(128)} %pad_add_fusion.3.refs_0_, ...), custom_call_target="tpu_custom_call", output_to_operand_aliasing={{0}: (6, {}), {1}: (7, {}), {2}: (8, {}), {3}: (9, {}), {4}... | custom-call | flops 1145044992 | bytes 12000000 | tf_op jit(solution)/shard_map/attend_forward/pallas_call | solution.py:374
  109.0 8.6 %feed_forward.11 = (bf16[4,208,3072]{2,1,0:T(8,128)(2,1)}, bf16[4,208,3072]{2,1,0:T(8,128)(2,1)}, bf16[4,208,768]{2,1,0:T(8,128)(2,1)}, bf16[4,208,768]{2,1,0:T(...) custom-call(s32[2]{0:T(128)} %pad_add_fusion.3.refs_0_, ...), custom_call_target="tpu_custom_call", output_to_operand_aliasing={{0}: (7, {}), {1}: (8, {}), {2}: (9, {}), {3}: (10, {}), {4... | custom-call | flops 1962934272 | bytes 12000000 | tf_op jit(solution)/shard_map/feed_forward/pallas_call | solution.py:374
  123.4 4.7 feed_forward.13
  129.7 4.4 feed_forward.14
  141.0 7.8 %attend_backward.8 = (bf16[4,208,768]{2,1,0:T(8,128)(2,1)}, bf16[4,208,2304]{2,1,0:T(8,128)(2,1)}, bf16[4,12,208,256]{3,2,1,0:T(8,128)(2,1)}, bf16[4,208,768]{2,...) custom-call(s32[2]{0:T(128)} %pad_add_fusion.2.refs_0_, ...), custom_call_target="tpu_custom_call" | custom-call | flops 1308622848 | bytes 12000000 | tf_op jit(solution)/shard_map/attend_backward/pallas_call | solution.py:374
  151.0 5.6 attend_backward.9
  166.5 8.0 %collective-permute-done.11.refs_1_ = bf16[208,768]{1,0:T(8,128)(2,1)S(1)} collective-permute-done((bf16[208,768]{1,0:T(8,128)(2,1)}, bf16[208,768]{1,0:T(8,128)(2,1)S(1)}, u32[]{:S(2)}, u32[]{:S(2)}) %collective-permute-start.11) | collective-permute-done | bytes 319520 | tf_op jit(solution)/shard_map/ppermute | solution.py:425
  175.1 9.4 %feed_backward.12 = (bf16[4,208,3072]{2,1,0:T(8,128)(2,1)}, bf16[4,208,3072]{2,1,0:T(8,128)(2,1)}, bf16[4,208,768]{2,1,0:T(8,128)(2,1)}, bf16[4,208,768]{2,1,0:T...) custom-call(s32[2]{0:T(128)} %pad_add_fusion.3.refs_0_, ...), custom_call_target="tpu_custom_call", output_to_operand_aliasing={{0}: (8, {}), {1}: (9, {}), {2}: (10, {}), {3}: (11, {}), {... | custom-call | flops 1962934272 | bytes 12000000 | tf_op jit(solution)/shard_map/feed_backward/pallas_call | solution.py:374
  184.6 9.1 %attend_backward.12 = (bf16[4,208,768]{2,1,0:T(8,128)(2,1)}, bf16[4,208,2304]{2,1,0:T(8,128)(2,1)}, bf16[4,12,208,256]{3,2,1,0:T(8,128)(2,1)}, bf16[4,208,768]{2...) custom-call(s32[2]{0:T(128)} %pad_add_fusion.3.refs_0_, ...), custom_call_target="tpu_custom_call", output_to_operand_aliasing={{0}: (7, {}), {1}: (8, {}), {2}: (9, {}), {3}: (10, {}), {4... | custom-call | flops 1308622848 | bytes 12000000 | tf_op jit(solution)/shard_map/attend_backward/pallas_call | solution.py:374
  194.8 9.4 %feed_backward.13 = (bf16[4,208,3072]{2,1,0:T(8,128)(2,1)}, bf16[4,208,3072]{2,1,0:T(8,128)(2,1)}, bf16[4,208,768]{2,1,0:T(8,128)(2,1)}, bf16[4,208,768]{2,1,0:T...) custom-call(s32[2]{0:T(128)} %pad_add_fusion.3.refs_0_, ...), custom_call_target="tpu_custom_call", output_to_operand_aliasing={{0}: (8, {}), {1}: (9, {}), {2}: (10, {}), {3}: (11, {}), {... | custom-call | flops 1962934272 | bytes 12000000 | tf_op jit(solution)/shard_map/feed_backward/pallas_call | solution.py:374
  204.3 8.7 %attend_backward.13 = (bf16[4,208,768]{2,1,0:T(8,128)(2,1)}, bf16[4,208,2304]{2,1,0:T(8,128)(2,1)}, bf16[4,12,208,256]{3,2,1,0:T(8,128)(2,1)}, bf16[4,208,768]{2...) custom-call(s32[2]{0:T(128)} %pad_add_fusion.3.refs_0_, ...), custom_call_target="tpu_custom_call", output_to_operand_aliasing={{0}: (7, {}), {1}: (8, {}), {2}: (9, {}), {3}: (10, {}), {4... | custom-call | flops 1308622848 | bytes 12000000 | tf_op jit(solution)/shard_map/attend_backward/pallas_call | solution.py:374
  214.3 9.4 %feed_backward.14 = (bf16[4,208,3072]{2,1,0:T(8,128)(2,1)}, bf16[4,208,3072]{2,1,0:T(8,128)(2,1)}, bf16[4,208,768]{2,1,0:T(8,128)(2,1)}, bf16[4,208,768]{2,1,0:T...) custom-call(s32[2]{0:T(128)} %pad_add_fusion.3.refs_0_, ...), custom_call_target="tpu_custom_call", output_to_operand_aliasing={{0}: (8, {}), {1}: (9, {}), {2}: (10, {}), {3}: (11, {}), {... | custom-call | flops 1962934272 | bytes 12000000 | tf_op jit(solution)/shard_map/feed_backward/pallas_call | solution.py:374
  223.7 8.9 %attend_backward.14 = (bf16[4,208,768]{2,1,0:T(8,128)(2,1)}, bf16[4,208,2304]{2,1,0:T(8,128)(2,1)}, bf16[4,12,208,256]{3,2,1,0:T(8,128)(2,1)}, bf16[4,208,768]{2...) custom-call(s32[2]{0:T(128)} %pad_add_fusion.3.refs_0_, ...), custom_call_target="tpu_custom_call", output_to_operand_aliasing={{0}: (7, {}), {1}: (8, {}), {2}: (9, {}), {3}: (10, {}), {4... | custom-call | flops 1308622848 | bytes 12000000 | tf_op jit(solution)/shard_map/attend_backward/pallas_call | solution.py:374
  234.0 9.5 %feed_backward.15 = (bf16[4,208,3072]{2,1,0:T(8,128)(2,1)}, bf16[4,208,3072]{2,1,0:T(8,128)(2,1)}, bf16[4,208,768]{2,1,0:T(8,128)(2,1)}, bf16[4,208,768]{2,1,0:T...) custom-call(s32[2]{0:T(128)} %pad_add_fusion.3.refs_0_, ...), custom_call_target="tpu_custom_call", output_to_operand_aliasing={{0}: (8, {}), {1}: (9, {}), {2}: (10, {}), {3}: (11, {}), {... | custom-call | flops 1962934272 | bytes 12000000 | tf_op jit(solution)/shard_map/feed_backward/pallas_call | solution.py:374
  243.5 8.9 %attend_backward.15 = (bf16[4,208,768]{2,1,0:T(8,128)(2,1)}, bf16[4,208,2304]{2,1,0:T(8,128)(2,1)}, bf16[4,12,208,256]{3,2,1,0:T(8,128)(2,1)}, bf16[4,208,768]{2...) custom-call(s32[2]{0:T(128)} %pad_add_fusion.3.refs_0_, ...), custom_call_target="tpu_custom_call", output_to_operand_aliasing={{0}: (7, {}), {1}: (8, {}), {2}: (9, {}), {3}: (10, {}), {4... | custom-call | flops 1308622848 | bytes 12000000 | tf_op jit(solution)/shard_map/attend_backward/pallas_call | solution.py:374
  302.2 5.0 convert_reduce_fusion
  325.5 4.3 collective-permute-done.32
  345.1 9.3 %bitcast_convert_fusion = bf16[768,3072]{1,0:T(8,128)(2,1)} fusion(bf16[4,208,768]{2,1,0:T(8,128)(2,1)S(1)} %copy-done.10, bf16[4,208,3072]{2,1,0:T(8,128)(2,1)} %get-tuple-element.474), kind=kOutput, calls=%fused_computation.33 | convolution fusion | flops 3928227840 | bytes 11108352 | tf_op jit(solution)/shard_map/dot_general | solution.py:29
  357.1 6.8 bitcast_convert_fusion.1
  663.8 34.2 %all-reduce.32 = (f32[1,8,768]{2,1,0:T(8,128)}, f32[1,12,732]{2,0,1:T(1,128)}) all-reduce(f32[1,8,768]{2,1,0:T(8,128)S(1)} %add_bitcast_fusion, f32[1,12,732]{2,0,1:T(1,128)S(1)} %broadcast_in_dim.109), channel_id=1, replica_groups=mesh['section'=4,'dp'=8] {'dp'}, use_global_device_ids=true, to_apply=%region_3.4 | all-reduce | flops 14928 | bytes 119424 | tf_op jit(solution)/shard_map/psum | solution.py:608
  707.5 7.3 %select_bitcast_fusion = f32[1,3072,768]{1,2,0:T(8,128)} fusion(bf16[768,3072]{1,0:T(8,128)(2,1)} %constant_dynamic-update-slice_fusion.24, pred[]{:T(512)S(6)} %eq.157), kind=kLoop, calls=%fused_computation.35 | loop fusion | flops 4718592 | bytes 14155777 | tf_op jit(solution)/shard_map/broadcast_in_dim | solution.py:623
  714.8 9.6 %copy.413 = f32[1,3072,768]{2,1,0:T(8,128)} copy(f32[1,3072,768]{1,2,0:T(8,128)} %select_bitcast_fusion) | data formatting | bytes 18874368
  724.4 8.0 %fusion.1 = f32[1,768,3072]{2,1,0:T(8,128)} fusion(bf16[768,3072]{1,0:T(8,128)(2,1)} %collective-permute-done.129, bf16[384,3072]{1,0:T(8,128)(2,1)} %collective-permute-done.71, bf16[384,3072]{1,0:T(8,128)(2,1)} %constant_dynamic-update-slice_fusion.16, pred[]{:T(512)S(6)} %eq.157), kind=kLoop, calls=%fused_computation.39 | loop fusion | flops 14155776 | bytes 18874368 | tf_op jit(solution)/shard_map/broadcast_in_dim | solution.py:622
  (546 shorter events, 438.2 us)
Async XLA Ops:
  0.6 45.8 %collective-permute-start.1 = (bf16[768,3072]{1,0:T(8,128)(2,1)}, bf16[768,3072]{1,0:T(8,128)(2,1)}, u32[]{:S(2)}, u32[]{:S(2)}) collective-permute-start(bf16[768,3072]{1,0:T(8,128)(2,1)} %bitcast.105), channel_id=1, source_target_pairs={{0,8},{8,0},{16,24},{24,16},{1,9},{9,1},{17,25},{25,17},{2,10},{10... | collective-permute-start | bytes 14155784 | tf_op jit(solution)/shard_map/ppermute | solution.py:425
  1.1 53.6 %collective-permute-start.3 = (bf16[3072,768]{1,0:T(8,128)(2,1)}, bf16[3072,768]{1,0:T(8,128)(2,1)}, u32[]{:S(2)}, u32[]{:S(2)}) collective-permute-start(bf16[3072,768]{1,0:T(8,128)(2,1)} %bitcast.138), channel_id=1, source_target_pairs={{8,0},{24,16},{9,1},{25,17},{10,2},{26,18},{11,3},{27,19},{12,4},{... | collective-permute-start | bytes 14155784 | tf_op jit(solution)/shard_map/ppermute | solution.py:425
  3.2 16.4 %collective-permute-start.2 = (f32[12,732]{1,0:T(8,128)S(1)}, f32[12,732]{1,0:T(8,128)S(1)}, u32[]{:S(2)}, u32[]{:S(2)}) collective-permute-start(f32[12,732]{1,0:T(8,128)S(1)} %bitcast.170), channel_id=1, source_target_pairs={{0,8},{16,24},{1,9},{17,25},{2,10},{18,26},{3,11},{19,27},{4,12},{... | collective-permute-start | bytes 105416 | tf_op jit(solution)/shard_map/ppermute | solution.py:425
  8.4 9.2 %collective-permute-start = (f32[8,768]{1,0:T(8,128)}, f32[8,768]{1,0:T(8,128)S(1)}, u32[]{:S(2)}, u32[]{:S(2)}) collective-permute-start(f32[8,768]{1,0:T(8,128)} %bitcast.171), channel_id=1, source_target_pairs={{0,8},{8,0},{16,24},{24,16},{1,9},{9,1},{17,25},{25,17},{2,10},{10... | collective-permute-start | bytes 73736 | tf_op jit(solution)/shard_map/ppermute | solution.py:425
  63.2 55.7 %collective-permute-start.7 = (bf16[208,768]{1,0:T(8,128)(2,1)}, bf16[208,768]{1,0:T(8,128)(2,1)S(1)}, u32[]{:S(2)}, u32[]{:S(2)}) collective-permute-start(bf16[208,768]{1,0:T(8,128)(2,1)} %get-tuple-element.294), channel_id=1, source_target_pairs={{0,16},{8,24},{1,17},{9,25},{2,18},{10,26},{3,19},{11,27},{4,20},{... | collective-permute-start | bytes 958472 | tf_op jit(solution)/shard_map/ppermute | solution.py:425
  81.5 40.3 %collective-permute-start.6 = (bf16[208,768]{1,0:T(8,128)(2,1)}, bf16[208,768]{1,0:T(8,128)(2,1)S(1)}, u32[]{:S(2)}, u32[]{:S(2)}) collective-permute-start(bf16[208,768]{1,0:T(8,128)(2,1)} %get-tuple-element.293), channel_id=1, source_target_pairs={{0,16},{8,24},{1,17},{9,25},{2,18},{10,26},{3,19},{11,27},{4,20},{... | collective-permute-start | bytes 958472 | tf_op jit(solution)/shard_map/ppermute | solution.py:425
  99.6 28.5 %collective-permute-start.5 = (bf16[208,768]{1,0:T(8,128)(2,1)}, bf16[208,768]{1,0:T(8,128)(2,1)S(1)}, u32[]{:S(2)}, u32[]{:S(2)}) collective-permute-start(bf16[208,768]{1,0:T(8,128)(2,1)} %get-tuple-element.292), channel_id=1, source_target_pairs={{0,16},{8,24},{1,17},{9,25},{2,18},{10,26},{3,19},{11,27},{4,20},{... | collective-permute-start | bytes 958472 | tf_op jit(solution)/shard_map/ppermute | solution.py:425
  117.6 16.5 %collective-permute-start.4 = (bf16[208,768]{1,0:T(8,128)(2,1)}, bf16[208,768]{1,0:T(8,128)(2,1)S(1)}, u32[]{:S(2)}, u32[]{:S(2)}) collective-permute-start(bf16[208,768]{1,0:T(8,128)(2,1)} %get-tuple-element.291), channel_id=1, source_target_pairs={{0,16},{8,24},{1,17},{9,25},{2,18},{10,26},{3,19},{11,27},{4,20},{... | collective-permute-start | bytes 958472 | tf_op jit(solution)/shard_map/ppermute | solution.py:425
  148.8 25.6 %collective-permute-start.11 = (bf16[208,768]{1,0:T(8,128)(2,1)}, bf16[208,768]{1,0:T(8,128)(2,1)S(1)}, u32[]{:S(2)}, u32[]{:S(2)}) collective-permute-start(bf16[208,768]{1,0:T(8,128)(2,1)} %get-tuple-element.408), channel_id=1, source_target_pairs={{16,0},{24,8},{17,1},{25,9},{18,2},{26,10},{19,3},{27,11},{20,4},{... | collective-permute-start | bytes 958472 | tf_op jit(solution)/shard_map/ppermute | solution.py:425
  156.6 37.5 %collective-permute-start.10 = (bf16[208,768]{1,0:T(8,128)(2,1)}, bf16[208,768]{1,0:T(8,128)(2,1)S(1)}, u32[]{:S(2)}, u32[]{:S(2)}) collective-permute-start(bf16[208,768]{1,0:T(8,128)(2,1)} %get-tuple-element.407), channel_id=1, source_target_pairs={{16,0},{24,8},{17,1},{25,9},{18,2},{26,10},{19,3},{27,11},{20,4},{... | collective-permute-start | bytes 958472 | tf_op jit(solution)/shard_map/ppermute | solution.py:425
  159.8 53.8 %collective-permute-start.9 = (bf16[208,768]{1,0:T(8,128)(2,1)}, bf16[208,768]{1,0:T(8,128)(2,1)S(1)}, u32[]{:S(2)}, u32[]{:S(2)}) collective-permute-start(bf16[208,768]{1,0:T(8,128)(2,1)} %get-tuple-element.406), channel_id=1, source_target_pairs={{16,0},{24,8},{17,1},{25,9},{18,2},{26,10},{19,3},{27,11},{20,4},{... | collective-permute-start | bytes 958472 | tf_op jit(solution)/shard_map/ppermute | solution.py:425
  165.2 68.1 %collective-permute-start.8 = (bf16[208,768]{1,0:T(8,128)(2,1)}, bf16[208,768]{1,0:T(8,128)(2,1)S(1)}, u32[]{:S(2)}, u32[]{:S(2)}) collective-permute-start(bf16[208,768]{1,0:T(8,128)(2,1)} %get-tuple-element.405), channel_id=1, source_target_pairs={{16,0},{24,8},{17,1},{25,9},{18,2},{26,10},{19,3},{27,11},{20,4},{... | collective-permute-start | bytes 958472 | tf_op jit(solution)/shard_map/ppermute | solution.py:425
  259.3 8.2 %collective-permute-start.14 = (bf16[384,3072]{1,0:T(8,128)(2,1)}, bf16[384,3072]{1,0:T(8,128)(2,1)}, u32[]{:S(2)}, u32[]{:S(2)}) collective-permute-start(bf16[384,3072]{1,0:T(8,128)(2,1)} %pad_maximum_fusion.2), channel_id=1, source_target_pairs={{0,8},{8,0},{16,24},{24,16},{1,9},{9,1},{17,25},{25,17},{2,10},{10... | collective-permute-start | bytes 7077896 | tf_op jit(solution)/shard_map/ppermute | solution.py:425
  290.9 8.7 %collective-permute-start.40 = (bf16[48,768]{1,0:T(8,128)(2,1)S(1)}, bf16[48,768]{1,0:T(8,128)(2,1)S(1)}, u32[]{:S(2)}, u32[]{:S(2)}) collective-permute-start(bf16[48,768]{1,0:T(8,128)(2,1)S(1)} %add_convert_fusion.35), channel_id=1, source_target_pairs={{0,1},{2,0},{4,2},{6,4},{7,6},{5,7},{3,5},{1,3},{8,9},{10,8},{12,1... | collective-permute-start | bytes 221192 | tf_op jit(solution)/shard_map/ppermute | solution.py:501
  338.4 70.1 %collective-permute-start.130 = (f32[8,768]{1,0:T(8,128)S(1)}, f32[8,768]{1,0:T(8,128)S(1)}, u32[]{:S(2)}, u32[]{:S(2)}) collective-permute-start(f32[8,768]{1,0:T(8,128)S(1)} %broadcast_select_fusion.9), channel_id=1, source_target_pairs={{0,8},{8,0},{16,24},{24,16},{1,9},{9,1},{17,25},{25,17},{2,10},{10... | collective-permute-start | bytes 73736 | tf_op jit(solution)/shard_map/ppermute | solution.py:425
  343.2 11.3 %collective-permute-start.23 = (bf16[48,768]{1,0:T(8,128)(2,1)S(1)}, bf16[48,768]{1,0:T(8,128)(2,1)S(1)}, u32[]{:S(2)}, u32[]{:S(2)}) collective-permute-start(bf16[48,768]{1,0:T(8,128)(2,1)S(1)} %get-tuple-element.557), channel_id=1, source_target_pairs={{0,1},{2,0},{4,2},{6,4},{7,6},{5,7},{3,5},{1,3},{8,9},{10,8},{12,1... | collective-permute-start | bytes 221192 | tf_op jit(solution)/shard_map/ppermute | solution.py:501
  354.5 61.7 %collective-permute-start.72 = (bf16[768,3072]{1,0:T(8,128)(2,1)}, bf16[768,3072]{1,0:T(8,128)(2,1)}, u32[]{:S(2)}, u32[]{:S(2)}) collective-permute-start(bf16[768,3072]{1,0:T(8,128)(2,1)} %bitcast_convert_fusion), channel_id=1, source_target_pairs={{0,8},{8,0},{16,24},{24,16},{1,9},{9,1},{17,25},{25,17},{2,10},{10... | collective-permute-start | bytes 14155784 | tf_op jit(solution)/shard_map/ppermute | solution.py:425
  355.5 8.4 %collective-permute-start.24 = (bf16[48,768]{1,0:T(8,128)(2,1)S(1)}, bf16[48,768]{1,0:T(8,128)(2,1)S(1)}, u32[]{:S(2)}, u32[]{:S(2)}) collective-permute-start(bf16[48,768]{1,0:T(8,128)(2,1)S(1)} %add_convert_fusion.53), channel_id=1, source_target_pairs={{0,1},{2,0},{4,2},{6,4},{7,6},{5,7},{3,5},{1,3},{8,9},{10,8},{12,1... | collective-permute-start | bytes 221192 | tf_op jit(solution)/shard_map/ppermute | solution.py:501
  408.5 33.3 %collective-permute-start.42 = (bf16[48,768]{1,0:T(8,128)(2,1)S(1)}, bf16[48,768]{1,0:T(8,128)(2,1)S(1)}, u32[]{:S(2)}, u32[]{:S(2)}) collective-permute-start(bf16[48,768]{1,0:T(8,128)(2,1)S(1)} %copy-done.32), channel_id=1, source_target_pairs={{0,1},{2,0},{4,2},{6,4},{7,6},{5,7},{3,5},{1,3},{8,9},{10,8},{12,1... | collective-permute-start | bytes 221192 | tf_op jit(solution)/shard_map/ppermute | solution.py:501
  410.1 10.1 %collective-permute-start.28 = (bf16[48,768]{1,0:T(8,128)(2,1)S(1)}, bf16[48,768]{1,0:T(8,128)(2,1)S(1)}, u32[]{:S(2)}, u32[]{:S(2)}) collective-permute-start(bf16[48,768]{1,0:T(8,128)(2,1)S(1)} %copy-done.34), channel_id=1, source_target_pairs={{0,1},{2,0},{4,2},{6,4},{7,6},{5,7},{3,5},{1,3},{8,9},{10,8},{12,1... | collective-permute-start | bytes 221192 | tf_op jit(solution)/shard_map/ppermute | solution.py:501
  435.3 9.5 %collective-permute-start.43 = (bf16[48,768]{1,0:T(8,128)(2,1)S(1)}, bf16[48,768]{1,0:T(8,128)(2,1)S(1)}, u32[]{:S(2)}, u32[]{:S(2)}) collective-permute-start(bf16[48,768]{1,0:T(8,128)(2,1)S(1)} %get-tuple-element.514), channel_id=1, source_target_pairs={{0,2},{2,4},{4,6},{6,7},{7,5},{5,3},{3,1},{1,0},{8,10},{10,12},{12... | collective-permute-start | bytes 221192 | tf_op jit(solution)/shard_map/ppermute | solution.py:507
  439.2 7.9 %collective-permute-start.75 = (bf16[96,768]{1,0:T(8,128)(2,1)S(1)}, bf16[96,768]{1,0:T(8,128)(2,1)S(1)}, u32[]{:S(2)}, u32[]{:S(2)}) collective-permute-start(bf16[96,768]{1,0:T(8,128)(2,1)S(1)} %get-tuple-element.542), channel_id=1, source_target_pairs={{0,2},{2,4},{4,6},{6,7},{7,5},{5,3},{3,1},{1,0},{8,10},{10,12},{12... | collective-permute-start | bytes 442376 | tf_op jit(solution)/shard_map/ppermute | solution.py:501
  453.6 8.9 %collective-permute-start.46 = (bf16[48,768]{1,0:T(8,128)(2,1)S(1)}, bf16[48,768]{1,0:T(8,128)(2,1)S(1)}, u32[]{:S(2)}, u32[]{:S(2)}) collective-permute-start(bf16[48,768]{1,0:T(8,128)(2,1)S(1)} %get-tuple-element.508), channel_id=1, source_target_pairs={{0,1},{2,0},{4,2},{6,4},{7,6},{5,7},{3,5},{1,3},{8,9},{10,8},{12,1... | collective-permute-start | bytes 221192 | tf_op jit(solution)/shard_map/ppermute | solution.py:507
  463.6 9.8 %collective-permute-start.48 = (bf16[48,768]{1,0:T(8,128)(2,1)S(1)}, bf16[48,768]{1,0:T(8,128)(2,1)S(1)}, u32[]{:S(2)}, u32[]{:S(2)}) collective-permute-start(bf16[48,768]{1,0:T(8,128)(2,1)S(1)} %collective-permute-done.44), channel_id=1, source_target_pairs={{0,1},{2,0},{4,2},{6,4},{7,6},{5,7},{3,5},{1,3},{8,9},{10,8},{12,1... | collective-permute-start | bytes 221192 | tf_op jit(solution)/shard_map/ppermute | solution.py:507
  464.8 9.2 %collective-permute-start.49 = (bf16[48,768]{1,0:T(8,128)(2,1)S(1)}, bf16[48,768]{1,0:T(8,128)(2,1)S(1)}, u32[]{:S(2)}, u32[]{:S(2)}) collective-permute-start(bf16[48,768]{1,0:T(8,128)(2,1)S(1)} %collective-permute-done.45), channel_id=1, source_target_pairs={{0,2},{2,4},{4,6},{6,7},{7,5},{5,3},{3,1},{1,0},{8,10},{10,12},{12... | collective-permute-start | bytes 221192 | tf_op jit(solution)/shard_map/ppermute | solution.py:507
  474.1 189.6 %collective-permute-start.131 = (f32[12,732]{1,0:T(8,128)S(1)}, f32[12,732]{1,0:T(8,128)S(1)}, u32[]{:S(2)}, u32[]{:S(2)}) collective-permute-start(f32[12,732]{1,0:T(8,128)S(1)} %maximum_multiply_fusion), channel_id=1, source_target_pairs={{8,0},{24,16},{9,1},{25,17},{10,2},{26,18},{11,3},{27,19},{12,4},{... | collective-permute-start | bytes 105416 | tf_op jit(solution)/shard_map/ppermute | solution.py:425
  476.0 222.0 %collective-permute-start.13 = (bf16[4,208,768]{2,1,0:T(8,128)(2,1)}, bf16[4,208,768]{2,1,0:T(8,128)(2,1)}, u32[]{:S(2)}, u32[]{:S(2)}) collective-permute-start(bf16[4,208,768]{2,1,0:T(8,128)(2,1)} %broadcast_select_fusion.2), channel_id=1, source_target_pairs={{0,8},{8,0},{16,24},{24,16},{1,9},{9,1},{17,25},{25,17},{2,10},{10... | collective-permute-start | bytes 3833864 | tf_op jit(solution)/shard_map/ppermute | solution.py:425
  477.2 226.6 %collective-permute-start.12 = (bf16[4,208,768]{2,1,0:T(8,128)(2,1)}, bf16[4,208,768]{2,1,0:T(8,128)(2,1)}, u32[]{:S(2)}, u32[]{:S(2)}) collective-permute-start(bf16[4,208,768]{2,1,0:T(8,128)(2,1)} %broadcast_select_fusion.6), channel_id=1, source_target_pairs={{0,8},{8,0},{16,24},{24,16},{1,9},{9,1},{17,25},{25,17},{2,10},{10... | collective-permute-start | bytes 3833864 | tf_op jit(solution)/shard_map/ppermute | solution.py:425
  485.4 8.7 %collective-permute-start.86 = (bf16[96,768]{1,0:T(8,128)(2,1)S(1)}, bf16[96,768]{1,0:T(8,128)(2,1)S(1)}, u32[]{:S(2)}, u32[]{:S(2)}) collective-permute-start(bf16[96,768]{1,0:T(8,128)(2,1)S(1)} %get-tuple-element.525), channel_id=1, source_target_pairs={{0,1},{2,0},{4,2},{6,4},{7,6},{5,7},{3,5},{1,3},{8,9},{10,8},{12,1... | collective-permute-start | bytes 442376 | tf_op jit(solution)/shard_map/ppermute | solution.py:501
  487.7 8.1 %collective-permute-start.93 = (bf16[96,768]{1,0:T(8,128)(2,1)S(1)}, bf16[96,768]{1,0:T(8,128)(2,1)S(1)}, u32[]{:S(2)}, u32[]{:S(2)}) collective-permute-start(bf16[96,768]{1,0:T(8,128)(2,1)S(1)} %get-tuple-element.524), channel_id=1, source_target_pairs={{0,2},{2,4},{4,6},{6,7},{7,5},{5,3},{3,1},{1,0},{8,10},{10,12},{12... | collective-permute-start | bytes 442376 | tf_op jit(solution)/shard_map/ppermute | solution.py:501
  582.2 142.2 %collective-permute-start.129 = (bf16[768,3072]{1,0:T(8,128)(2,1)}, bf16[768,3072]{1,0:T(8,128)(2,1)}, u32[]{:S(2)}, u32[]{:S(2)}) collective-permute-start(bf16[768,3072]{1,0:T(8,128)(2,1)} %constant_dynamic-update-slice_fusion.24), channel_id=1, source_target_pairs={{0,8},{16,24},{1,9},{17,25},{2,10},{18,26},{3,11},{19,27},{4,12},{... | collective-permute-start | bytes 14155784 | tf_op jit(solution)/shard_map/ppermute | solution.py:425
  662.4 62.0 %collective-permute-start.71 = (bf16[384,3072]{1,0:T(8,128)(2,1)}, bf16[384,3072]{1,0:T(8,128)(2,1)}, u32[]{:S(2)}, u32[]{:S(2)}) collective-permute-start(bf16[384,3072]{1,0:T(8,128)(2,1)} %constant_dynamic-update-slice_fusion.16), channel_id=1, source_target_pairs={{8,0},{24,16},{9,1},{25,17},{10,2},{26,18},{11,3},{27,19},{12,4},{... | collective-permute-start | bytes 7077896 | tf_op jit(solution)/shard_map/ppermute | solution.py:425
  (144 other events, 944.3 us)
